TPU v7x, 32 devices: a whole 2x2x4 slice. The times are simulated.
32 devices in a mesh: shard: 4 (over z), context: 4 (over x, core), tensor: 2 (over y).
Axes of the slice: x: 2, y: 2, z: 4, core: 2. Of those that a mesh axis runs over, the one named last changes fastest.
Arguments:
- inputs: float32 [4, 512, 1024], P('shard', 'context'), may hold values from -8.5 to 8.5
- attn_gain: bfloat16 [1024], P(('shard', 'context')), may hold values from 0.5 to 1.5
- query_weight: bfloat16 [1024, 1024], P(('shard', 'context'), 'tensor'), may hold values from -0.1875 to 0.1875
- key_weight: bfloat16 [1024, 512], P(('shard', 'context'), 'tensor'), may hold values from -0.1875 to 0.1875
- value_matrix: bfloat16 [1024, 512], P(('shard', 'context'), 'tensor'), may hold values from -0.1875 to 0.1875
- output_weight: bfloat16 [1024, 1024], P(('shard', 'context'), 'tensor'), may hold values from -4 to 4
- ffn_gain: bfloat16 [1024], P(('shard', 'context')), may hold values from 0.5 to 1.5
- gate_weight: bfloat16 [1024, 16, 512], P(('shard', 'context'), None, 'tensor'), may hold values from -0.1875 to 0.1875
- up_weight: bfloat16 [1024, 16, 512], P(('shard', 'context'), None, 'tensor'), may hold values from -0.1875 to 0.1875
- down_weight: bfloat16 [1024, 16, 512], P(('shard', 'context'), None, 'tensor'), may hold values from -2 to 2
- routes: int32 [4, 512, 8], P('shard', 'context'), may hold values from 0 to 15, all different within a row; in each aligned block of 128 rows (0 to 127, 128 to 255, ..., all dimensions but the last counted through in order) at most 80 rows name the same one
- route_weights: float32 [4, 512, 8], P('shard', 'context'), may hold values from 0.05 to 0.25
- cotangent: float32 [4, 512, 1024], P('shard', 'context'), may hold values from -6 to 6
Outputs:
- output: float32 [4, 512, 1024], P('shard', 'context')
- grad_input: float32 [4, 512, 1024], P('shard', 'context')
- grad_attn_gain: float32 [1024], P(('shard', 'context'))
- grad_query_weight: float32 [1024, 1024], P(('shard', 'context'), 'tensor')
- grad_key_weight: float32 [1024, 512], P(('shard', 'context'), 'tensor')
- grad_value_weight: float32 [1024, 512], P(('shard', 'context'), 'tensor')
- grad_output_weight: float32 [1024, 1024], P(('shard', 'context'), 'tensor')
- grad_ffn_gain: float32 [1024], P(('shard', 'context'))
- grad_gate_weight: float32 [1024, 16, 512], P(('shard', 'context'), None, 'tensor')
- grad_up_weight: float32 [1024, 16, 512], P(('shard', 'context'), None, 'tensor')
- grad_down_weight: float32 [1024, 16, 512], P(('shard', 'context'), None, 'tensor')
Inputs may be any that keep to these rules, and one draw needn't show every extreme that they name: `routes`: each token names 8 different experts. Within each aligned block of 128 positions of a sequence no expert is named more than 80 times, and some block names some expert exactly 80 times.
All inputs are finite; a program needn't handle non-finite values.
Results may differ from a plain program's by a relative error of at most 0.012.
Values may be sent and summed in bfloat16 or wider, within the bound.
A program may use at most 128 MiB of HBM per device.

v0:
```python
import jax
import jax.numpy as jnp
from jax import lax
from jax.sharding import PartitionSpec as P

HEAD_DIM = 64
CAP = 80


EPS = 1e-06
SCORE_SCALE = 0.015625
RESIDUAL_SCALE = 0.22
ROPE_BASE = 10000.0
NEG = -1e30


def rope_tables(positions, head_width):
    half_width = head_width // 2
    frequency = ROPE_BASE ** (-2.0 * jnp.arange(half_width, dtype=jnp.float32) / head_width)
    angles = positions.astype(jnp.float32)[:, None] * frequency[None, :]
    angles = jnp.concatenate([angles, angles], axis=1)
    return (jnp.cos(angles), jnp.sin(angles))


def apply_rotary(value_rows, cosine_table, rotary_sine_values):
    half_width = value_rows.shape[-1] // 2
    first_half = value_rows[..., :half_width]
    second_half = value_rows[..., half_width:]
    turned = jnp.concatenate([-second_half, first_half], axis=-1)
    return value_rows * cosine_table[:, None, :] + turned * rotary_sine_values[:, None, :]


def reverse_rotary(grads_in, cosine_table, rotary_sine_values):
    half_width = grads_in.shape[-1] // 2
    product = grads_in * rotary_sine_values[:, None, :]
    turned = jnp.concatenate([product[..., half_width:], -product[..., :half_width]], axis=-1)
    return grads_in * cosine_table[:, None, :] + turned


def inverse_rms(value_rows):
    return lax.rsqrt(jnp.mean(value_rows * value_rows, axis=-1, keepdims=True) + EPS)


def norm_backward(grad_normed, source, factor, gain_vector):
    scaled = grad_normed * gain_vector
    return factor * scaled - source * (factor * factor * factor) * jnp.mean(
        scaled * source, axis=-1, keepdims=True
    )


def contract_rows(left, right):
    return lax.dot_general(
        left, right, (((0,), (0,)), ((), ())), preferred_element_type=jnp.float32
    )


def contract_cols(left, right):
    return lax.dot_general(
        left, right, (((1,), (1,)), ((), ())), preferred_element_type=jnp.float32
    )


def expert_math(disp_slots, grad_slots, gate_mat, up_mat, down_mat):
    gate_act = jnp.einsum("ecd,def->ecf", disp_slots, gate_mat, preferred_element_type=jnp.float32)
    up_act = jnp.einsum("ecd,def->ecf", disp_slots, up_mat, preferred_element_type=jnp.float32)
    sigma = jax.nn.sigmoid(gate_act)
    swish = gate_act * sigma
    activated = (swish * up_act).astype(jnp.bfloat16)
    expert_out = jnp.einsum("ecf,def->ecd", activated, down_mat, preferred_element_type=jnp.float32)
    grad_act = jnp.einsum("ecd,def->ecf", grad_slots, down_mat, preferred_element_type=jnp.float32)
    grad_swish = sigma * (1.0 + gate_act * (1.0 - sigma))
    grad_gate = (grad_act * up_act * grad_swish).astype(jnp.bfloat16)
    grad_up = (grad_act * swish).astype(jnp.bfloat16)
    grad_disp = jnp.einsum(
        "ecf,def->ecd", grad_gate, gate_mat, preferred_element_type=jnp.float32
    ) + jnp.einsum("ecf,def->ecd", grad_up, up_mat, preferred_element_type=jnp.float32)
    return (expert_out, grad_disp, grad_gate, grad_up, activated)


def natural_order(gathered, shard_count, context_count):
    shape = gathered.shape
    split = gathered.reshape((context_count, shard_count, -1) + shape[1:])
    return jnp.swapaxes(split, 0, 1).reshape(shape)


def body(
    inputs,
    attn_gain,
    query_weight,
    key_weight,
    value_matrix,
    output_weight,
    ffn_gain,
    gate_weight,
    up_weight,
    down_weight,
    routes,
    route_weights,
    cotangent,
):
    gains_attn, gains_ffn, query_full, key_full, value_full, output_full = (
        lax.all_gather(attn_gain, ("shard", "context"), axis=0, tiled=True),
        lax.all_gather(ffn_gain, ("shard", "context"), axis=0, tiled=True),
        lax.all_gather(query_weight, ("shard", "context"), axis=0, tiled=True),
        lax.all_gather(key_weight, ("shard", "context"), axis=0, tiled=True),
        lax.all_gather(value_matrix, ("shard", "context"), axis=0, tiled=True),
        lax.all_gather(output_weight, ("shard", "context"), axis=0, tiled=True),
    )
    tokens = inputs[0]
    length = tokens.shape[0]
    model_width = tokens.shape[1]
    head_size = HEAD_DIM
    kv_heads = key_full.shape[1] // head_size
    query_group_count = query_full.shape[1] // key_full.shape[1]
    experts = gate_weight.shape[1]
    top_count = routes.shape[2]
    capacity = CAP
    context_count_all = lax.axis_size("context")
    gain_attn = gains_attn.astype(jnp.float32)
    gain_ffn = gains_ffn.astype(jnp.float32)
    positions = lax.axis_index("context") * length + jnp.arange(length, dtype=jnp.int32)
    cosine_table, rotary_sine_values = rope_tables(positions, head_size)
    scale_one = inverse_rms(tokens)
    normed_one = (tokens * scale_one * gain_attn).astype(jnp.bfloat16)
    query_lin = jnp.dot(normed_one, query_full, preferred_element_type=jnp.float32)
    linear_keys = jnp.dot(normed_one, key_full, preferred_element_type=jnp.float32)
    value_rows = jnp.dot(normed_one, value_full, preferred_element_type=jnp.float32).astype(
        jnp.bfloat16
    )
    query_rows = apply_rotary(
        query_lin.reshape(length, kv_heads * query_group_count, head_size),
        cosine_table,
        rotary_sine_values,
    ).astype(jnp.bfloat16)
    query_rows = query_rows.reshape(length, kv_heads, query_group_count, head_size)
    key_rows = apply_rotary(
        linear_keys.reshape(length, kv_heads, head_size), cosine_table, rotary_sine_values
    ).astype(jnp.bfloat16)
    key_rows = key_rows.reshape(length, kv_heads * head_size)

    def block_scores(key_piece, start):
        count = key_piece.shape[0]
        key_block = key_piece.reshape(count, kv_heads, head_size)
        scores = (
            jnp.einsum("tkgd,skd->kgts", query_rows, key_block, preferred_element_type=jnp.float32)
            * SCORE_SCALE
        )
        key_pos = start + jnp.arange(count, dtype=jnp.int32)
        visible = key_pos[None, :] <= positions[:, None]
        return (key_block, scores, visible)

    running_max = jnp.full((kv_heads, query_group_count, length), NEG, jnp.float32)
    key_piece = lax.all_gather(key_rows, "context", axis=0, tiled=True)
    value_piece = lax.all_gather(value_rows, "context", axis=0, tiled=True)
    key_block, scores, visible = block_scores(key_piece, jnp.int32(0))
    masked = jnp.where(visible, scores, NEG)
    new_max = jnp.maximum(running_max, jnp.max(masked, axis=-1))
    weights_exp = jnp.where(visible, jnp.exp(scores - new_max[..., None]), 0.0)
    running_sum = jnp.sum(weights_exp, axis=-1)
    attend_keys_all = key_piece
    attend_values_all = value_piece
    log_total = new_max + jnp.log(running_sum)

    def context_block(block_index, accum):
        start = block_index * length
        key_piece = lax.dynamic_slice_in_dim(attend_keys_all, start, length, 0)
        value_piece = lax.dynamic_slice_in_dim(attend_values_all, start, length, 0)
        key_block, scores, visible = block_scores(key_piece, start)
        soft_b = jnp.where(visible, jnp.exp(scores - log_total[..., None]), 0.0).astype(
            jnp.bfloat16
        )
        value_block = value_piece.reshape(length, kv_heads, head_size)
        return accum + jnp.einsum(
            "kgts,skd->kgtd", soft_b, value_block, preferred_element_type=jnp.float32
        )

    accum = lax.fori_loop(
        0,
        context_count_all,
        context_block,
        jnp.zeros((kv_heads, query_group_count, length, head_size), jnp.float32),
    )
    attended_context = (
        jnp.transpose(accum, (2, 0, 1, 3))
        .reshape(length, kv_heads * query_group_count * head_size)
        .astype(jnp.bfloat16)
    )
    attn_part = contract_cols(attended_context, output_full)
    attn_out = lax.psum(attn_part, "tensor")
    hidden = tokens + RESIDUAL_SCALE * attn_out
    scale_two = inverse_rms(hidden)
    normed_two = (hidden * scale_two * gain_ffn).astype(jnp.bfloat16)
    flat_routes = routes[0].reshape(-1)
    onehot = (flat_routes[:, None] == jnp.arange(experts, dtype=jnp.int32)[None, :]).astype(
        jnp.int32
    )
    slots = jnp.sum((jnp.cumsum(onehot, axis=0) - onehot) * onehot, axis=1)
    slot_index = flat_routes * capacity + slots
    dispatched = (
        jnp.zeros((experts * capacity, model_width), jnp.bfloat16)
        .at[slot_index]
        .set(jnp.repeat(normed_two, top_count, axis=0))
        .reshape(experts, capacity, model_width)
    )
    grad_out = cotangent[0]
    weights_route = route_weights[0]
    grad_moe = RESIDUAL_SCALE * grad_out
    spread_rows = (
        (weights_route[..., None] * grad_moe[:, None, :])
        .reshape(length * top_count, model_width)
        .astype(jnp.bfloat16)
    )
    grad_buffer = (
        jnp.zeros((experts * capacity, model_width), jnp.bfloat16)
        .at[slot_index]
        .set(spread_rows)
        .reshape(experts, capacity, model_width)
    )
    shard_count = lax.axis_size("shard")
    context_count = lax.axis_size("context")
    owner_gate, owner_up, owner_down = (
        lax.all_to_all(gate_weight, "shard", split_axis=1, concat_axis=0, tiled=True),
        lax.all_to_all(up_weight, "shard", split_axis=1, concat_axis=0, tiled=True),
        lax.all_to_all(down_weight, "shard", split_axis=1, concat_axis=0, tiled=True),
    )
    context_gate, context_up, context_down = (
        lax.all_gather(owner_gate, "context", axis=0, tiled=True),
        lax.all_gather(owner_up, "context", axis=0, tiled=True),
        lax.all_gather(owner_down, "context", axis=0, tiled=True),
    )
    own_gate = natural_order(context_gate, shard_count, context_count)
    own_up = natural_order(context_up, shard_count, context_count)
    own_down = natural_order(context_down, shard_count, context_count)
    recv_disp, recv_grad = (
        lax.all_to_all(dispatched, "shard", split_axis=0, concat_axis=1, tiled=True),
        lax.all_to_all(grad_buffer, "shard", split_axis=0, concat_axis=1, tiled=True),
    )
    local_out, local_grad, local_gate_grad, local_up_grad, local_act = expert_math(
        recv_disp, recv_grad, own_gate, own_up, own_down
    )
    expert_out, grad_disp = (
        lax.all_to_all(local_out, "shard", split_axis=1, concat_axis=0, tiled=True),
        lax.all_to_all(local_grad, "shard", split_axis=1, concat_axis=0, tiled=True),
    )
    term_gate = jnp.einsum(
        "ecd,ecf->def", recv_disp, local_gate_grad, preferred_element_type=jnp.float32
    )
    term_up = jnp.einsum(
        "ecd,ecf->def", recv_disp, local_up_grad, preferred_element_type=jnp.float32
    )
    term_down = jnp.einsum("ecd,ecf->def", recv_grad, local_act, preferred_element_type=jnp.float32)
    stacked = jnp.stack([term_gate, term_up, term_down], axis=1)
    split_terms = stacked.reshape((shard_count, context_count, -1) + stacked.shape[1:])
    reordered = jnp.swapaxes(split_terms, 0, 1).reshape(stacked.shape)
    context_sums = lax.psum_scatter(reordered, "context", scatter_dimension=0, tiled=True)
    expert_sums = lax.all_to_all(context_sums, "shard", split_axis=0, concat_axis=2, tiled=True)
    picked = expert_out.reshape(experts * capacity, model_width)[slot_index].reshape(
        length, top_count, model_width
    )
    moe_part = jnp.sum(picked * weights_route[..., None], axis=1)
    normed_two_part = jnp.sum(
        grad_disp.reshape(experts * capacity, model_width)[slot_index].reshape(
            length, top_count, model_width
        ),
        axis=1,
    )
    moe, grad_normed_two = lax.psum((moe_part, normed_two_part), "tensor")
    output = hidden + RESIDUAL_SCALE * moe
    term_ffn_gain = jnp.sum(grad_normed_two * hidden * scale_two, axis=0)
    grad_hidden = grad_out + norm_backward(grad_normed_two, hidden, scale_two, gain_ffn)
    grad_attn = (RESIDUAL_SCALE * grad_hidden).astype(jnp.bfloat16)
    term_output = contract_rows(grad_attn, attended_context)
    context_gradient = jnp.dot(grad_attn, output_full, preferred_element_type=jnp.float32).astype(
        jnp.bfloat16
    )
    grad_context_heads = context_gradient.reshape(length, kv_heads, query_group_count, head_size)
    softmax_delta = jnp.sum(
        grad_context_heads.astype(jnp.float32)
        * attended_context.reshape(length, kv_heads, query_group_count, head_size).astype(
            jnp.float32
        ),
        axis=-1,
    )
    softmax_delta = jnp.transpose(softmax_delta, (1, 2, 0))
    key_piece = lax.all_gather(key_rows, "context", axis=0, tiled=True)
    value_piece = lax.all_gather(value_rows, "context", axis=0, tiled=True)
    count = key_piece.shape[0]
    key_block, scores, visible = block_scores(key_piece, jnp.int32(0))
    soft = jnp.where(visible, jnp.exp(scores - log_total[..., None]), 0.0)
    value_block = value_piece.reshape(count, kv_heads, head_size)
    value_term = jnp.einsum(
        "kgts,tkgd->skd",
        soft.astype(jnp.bfloat16),
        grad_context_heads,
        preferred_element_type=jnp.float32,
    )
    grad_soft = jnp.einsum(
        "tkgd,skd->kgts", grad_context_heads, value_block, preferred_element_type=jnp.float32
    )
    grad_scores = (soft * (grad_soft - softmax_delta[..., None])).astype(jnp.bfloat16)
    grad_query = SCORE_SCALE * jnp.einsum(
        "kgts,skd->tkgd", grad_scores, key_block, preferred_element_type=jnp.float32
    )
    key_term = SCORE_SCALE * jnp.einsum(
        "kgts,tkgd->skd", grad_scores, query_rows, preferred_element_type=jnp.float32
    )
    grad_keys_all = key_term.reshape(count, kv_heads * head_size)
    grad_values_all = value_term.reshape(count, kv_heads * head_size)
    grad_query, grad_keys_all, grad_values_all = (grad_query, grad_keys_all, grad_values_all)
    grad_keys_own, grad_values_own = (
        lax.psum_scatter(grad_keys_all, "context", scatter_dimension=0, tiled=True),
        lax.psum_scatter(grad_values_all, "context", scatter_dimension=0, tiled=True),
    )
    grad_query_lin = (
        reverse_rotary(
            grad_query.reshape(length, kv_heads * query_group_count, head_size),
            cosine_table,
            rotary_sine_values,
        )
        .reshape(length, kv_heads * query_group_count * head_size)
        .astype(jnp.bfloat16)
    )
    linear_key_gradient = (
        reverse_rotary(
            grad_keys_own.reshape(length, kv_heads, head_size), cosine_table, rotary_sine_values
        )
        .reshape(length, kv_heads * head_size)
        .astype(jnp.bfloat16)
    )
    value_gradient_second = grad_values_own.astype(jnp.bfloat16)
    term_query = contract_rows(normed_one, grad_query_lin)
    term_key = contract_rows(normed_one, linear_key_gradient)
    term_value = contract_rows(normed_one, value_gradient_second)
    normed_one_part = (
        contract_cols(grad_query_lin, query_full)
        + contract_cols(linear_key_gradient, key_full)
        + contract_cols(value_gradient_second, value_full)
    )
    grad_normed_one = lax.psum(normed_one_part, "tensor")
    term_attn_gain = jnp.sum(grad_normed_one * tokens * scale_one, axis=0)
    grad_input = grad_hidden + norm_backward(grad_normed_one, tokens, scale_one, gain_attn)
    sum_attn_gain, sum_query, sum_key, sum_value, sum_output, sum_ffn_gain = (
        lax.psum_scatter(term_attn_gain, ("shard", "context"), scatter_dimension=0, tiled=True),
        lax.psum_scatter(term_query, ("shard", "context"), scatter_dimension=0, tiled=True),
        lax.psum_scatter(term_key, ("shard", "context"), scatter_dimension=0, tiled=True),
        lax.psum_scatter(term_value, ("shard", "context"), scatter_dimension=0, tiled=True),
        lax.psum_scatter(term_output, ("shard", "context"), scatter_dimension=0, tiled=True),
        lax.psum_scatter(term_ffn_gain, ("shard", "context"), scatter_dimension=0, tiled=True),
    )
    return (
        output[None],
        grad_input[None],
        sum_attn_gain,
        sum_query,
        sum_key,
        sum_value,
        sum_output,
        sum_ffn_gain,
        expert_sums[:, 0],
        expert_sums[:, 1],
        expert_sums[:, 2],
    )


def solution(mesh):
    placed = (
        P("shard", "context", None),
        P(("shard", "context")),
        P(("shard", "context"), "tensor"),
        P(("shard", "context"), "tensor"),
        P(("shard", "context"), "tensor"),
        P(("shard", "context"), "tensor"),
        P(("shard", "context")),
        P(("shard", "context"), None, "tensor"),
        P(("shard", "context"), None, "tensor"),
        P(("shard", "context"), None, "tensor"),
        P("shard", "context", None),
        P("shard", "context", None),
        P("shard", "context", None),
    )
    return jax.shard_map(
        body,
        mesh=mesh,
        in_specs=placed,
        out_specs=(
            P("shard", "context", None),
            P("shard", "context", None),
            P(("shard", "context")),
            P(("shard", "context"), "tensor"),
            P(("shard", "context"), "tensor"),
            P(("shard", "context"), "tensor"),
            P(("shard", "context"), "tensor"),
            P(("shard", "context")),
            P(("shard", "context"), None, "tensor"),
            P(("shard", "context"), None, "tensor"),
            P(("shard", "context"), None, "tensor"),
        ),
        check_vma=False,
    )
```

profile of v0, /device:TPU:0, one launch (start us, length us, event | category | flops | bytes accessed | tf_op | source)
XLA Modules:
  0.0 990.9 jit_solution(8059755671351165740)
XLA Ops:
  19.7 34.1 %all-reduce.6 = (bf16[1024]{0:T(1024)(128)(2,1)S(1)}, bf16[1024]{0:T(1024)(128)(2,1)S(1)}) all-reduce(bf16[1024]{0:T(1024)(128)(2,1)S(1)} %dynamic-update-slice, bf16[1024]{0:T(1024)(128)(2,1)S(1)} %dynamic-update-slice.1), channel_id=1, replica_groups=mesh['shard'=4,'context'=4,'tensor'=2] {'shard','context'}, use_global_device_ids=true, to_apply=%add | all-reduce | flops 2048 | bytes 8192
  54.8 19.4 %all_gather.36 = bf16[1024,256]{1,0:T(8,128)(2,1)S(1)} all-gather(bf16[64,256]{1,0:T(8,128)(2,1)S(1)} %copy-done.46), channel_id=1, replica_groups=mesh['shard'=4,'context'=4,'tensor'=2] {'shard','context'}, dimensions={0}, use_global_device_ids=true | all-gather | bytes 557056 | tf_op jit(solution)/shard_map/all_gather | solution.py:105
  81.7 20.5 %all_gather.39 = bf16[1024,256]{1,0:T(8,128)(2,1)S(1)} all-gather(bf16[64,256]{1,0:T(8,128)(2,1)S(1)} %copy-done.47), channel_id=1, replica_groups=mesh['shard'=4,'context'=4,'tensor'=2] {'shard','context'}, dimensions={0}, use_global_device_ids=true | all-gather | bytes 557056 | tf_op jit(solution)/shard_map/all_gather | solution.py:106
  134.7 6.8 all-to-all-done.2
  145.1 7.5 scatter_custom_fusion.1
  152.7 6.7 all-to-all-done.3
  168.8 7.4 scatter_custom_fusion
  176.2 46.5 %all-to-all-done.5 = bf16[16,80,1024]{2,1,0:T(8,128)(2,1)S(1)} async-done(((bf16[16,80,1024]{2,1,0:T(8,128)(2,1)}), bf16[16,80,1024]{2,1,0:T(8,128)(2,1)S(1)}, u32[]{:S(2)}, u32[]{:S(2)}) %all-to-all-start.5) | async-done | bytes 2621472 | tf_op jit(solution)/shard_map/all_to_all | solution.py:236
  237.5 15.6 %all-gather.14.cloned.1.call-done = bf16[1024,4,256]{2,0,1:T(8,128)(2,1)} async-done(((bf16[256,4,256]{2,0,1:T(8,128)(2,1)}), bf16[1024,4,256]{2,0,1:T(8,128)(2,1)}) %all-gather.14.cloned.1.call-update) | async-done | bytes 2097168 | tf_op jit(solution)/shard_map/all_gather | solution.py:229
  256.2 30.0 %all-to-all-done = bf16[16,80,1024]{2,1,0:T(8,128)(2,1)} async-done(((bf16[16,80,1024]{2,1,0:T(8,128)(2,1)}), bf16[16,80,1024]{2,1,0:T(8,128)(2,1)}, u32[]{:S(2)}, u32[]{:S(2)}) %all-to-all-start) | async-done | bytes 2621472 | tf_op jit(solution)/shard_map/all_to_all | solution.py:235
  307.8 114.9 %all-to-all-done.6 = f32[4,320,1024]{2,0,1:T(4,128)} async-done(((f32[4,320,1024]{2,0,1:T(4,128)}), f32[4,320,1024]{2,0,1:T(4,128)}, u32[]{:S(2)}, u32[]{:S(2)}) %all-to-all-start.6) | async-done | bytes 5242912 | tf_op jit(solution)/shard_map/all_to_all | solution.py:243
  422.7 7.9 copy.131
  430.6 8.9 gather_fusion.1
  443.6 27.1 %all-reduce.13.cloned.1.call-done = f32[128,1024]{1,0:T(8,128)} async-done(((f32[128,1024]{1,0:T(8,128)}), f32[128,1024]{1,0:T(8,128)}) %all-reduce.13.cloned.1.call-update) | async-done | bytes 524304 | tf_op jit(solution)/shard_map/psum | solution.py:267
  516.0 11.4 %maximum_bitcast_fusion = f32[4,4,64,3,4,256]{5,2,0,1,4,3:T(8,128)} fusion(f32[4,4,64,1,4,256]{5,2,1,0,4,3:T(8,128)} %bitcast.330, f32[4,4,64,1,4,256]{5,2,1,0,4,3:T(8,128)} %bitcast.331, f32[4,4,64,1,4,256]{5,2,1,0,4,3:T(8,128)} %bitcast.332), kind=kLoop, calls=%fused_computation.23 | loop fusion | flops 6291456 | bytes 25165824 | tf_op jit(solution)/shard_map/transpose | solution.py:254
  527.4 11.4 %copy.140 = f32[4,4,64,3,4,256]{5,2,1,0,4,3:T(8,128)} copy(f32[4,4,64,3,4,256]{5,2,0,1,4,3:T(8,128)} %maximum_bitcast_fusion) | data formatting | bytes 25165824 | tf_op jit(solution)/shard_map/transpose | solution.py:254
  554.6 115.2 %all-to-all-done.4 = f32[4,320,1024]{2,0,1:T(4,128)} async-done(((f32[4,320,1024]{2,0,1:T(4,128)}), f32[4,320,1024]{2,0,1:T(4,128)}, u32[]{:S(2)}, u32[]{:S(2)}) %all-to-all-start.4) | async-done | bytes 5242912 | tf_op jit(solution)/shard_map/all_to_all | solution.py:242
  669.8 7.9 copy.126
  677.7 8.9 gather_fusion
  716.2 20.6 %all-reduce.15.cloned.1.call-done = (f32[128,1024]{1,0:T(8,128)}, f32[128,1024]{1,0:T(8,128)}) async-done(((f32[128,1024]{1,0:T(8,128)}, f32[128,1024]{1,0:T(8,128)}), (f32[128,1024]{1,0:T(8,128)}, f32[128,1024]{1,0:T(8,128)})) %all-reduce.15.cloned.1.call-update) | async-done | bytes 1048592 | tf_op jit(solution)/shard_map/psum | solution.py:267
  738.0 58.2 %all-reduce.4 = (f32[1024]{0:T(1024)S(1)}, f32[1024]{0:T(1024)S(1)}) all-reduce(f32[1024]{0:T(1024)S(1)} %get-tuple-element.215, f32[1024]{0:T(1024)S(1)} %get-tuple-element.213), channel_id=4, replica_groups=mesh['shard'=4,'context'=4,'tensor'=2] {'shard','context'}, use_global_device_ids=true, to_apply=%region_23.24.clone | all-reduce | flops 2048 | bytes 16384
  807.7 45.9 %reduce-scatter.16.cloned.1.call-done = f32[64,256]{1,0:T(8,128)} async-done(((f32[1024,256]{1,0:T(8,128)}), f32[64,256]{1,0:T(8,128)}) %reduce-scatter.16.cloned.1.call-update) | async-done | bytes 65552 | tf_op jit(solution)/shard_map/reduce_scatter | solution.py:346
  853.5 65.2 %reduce-scatter.12.cloned.1.call-done = f32[64,512]{1,0:T(8,128)} async-done(((f32[1024,512]{1,0:T(8,128)}), f32[64,512]{1,0:T(8,128)}) %reduce-scatter.12.cloned.1.call-update) | async-done | bytes 131088 | tf_op jit(solution)/shard_map/reduce_scatter | solution.py:344
  918.7 64.9 %reduce-scatter.18.cloned.1.call-done = f32[64,512]{1,0:T(8,128)} async-done(((f32[1024,512]{1,0:T(8,128)}), f32[64,512]{1,0:T(8,128)}) %reduce-scatter.18.cloned.1.call-update) | async-done | bytes 131088 | tf_op jit(solution)/shard_map/reduce_scatter | solution.py:347
  (306 shorter events, 215.2 us)
Async XLA Ops:
  8.1 100.4 %all-gather.6.cloned.1.call-start = ((), (), s32[]{:S(2)}) async-start(), calls=%async_computation.15 | async-start | bytes 1114112 | tf_op jit(solution)/shard_map/all_gather | solution.py:104
  10.8 111.9 %all-to-all-start.1 = ((bf16[64,16,256]{2,0,1:T(8,128)(2,1)}), bf16[64,16,256]{2,0,1:T(8,128)(2,1)}, u32[]{:S(2)}, u32[]{:S(2)}) async-start(bf16[64,16,256]{2,0,1:T(8,128)(2,1)} %copy.116), calls=%async_computation.1 | async-start | bytes 1048576 | tf_op jit(solution)/shard_map/all_to_all | solution.py:222
  17.1 101.8 %all-gather.8.cloned.1.call-start = ((), (), s32[]{:S(2)}) async-start(), calls=%async_computation.16 | async-start | bytes 1114112 | tf_op jit(solution)/shard_map/all_gather | solution.py:107
  17.9 148.1 %all-reduce.11.cloned.1.call-start = ((), (), s32[]{:S(2)}) async-start(), calls=%async_computation.17 | async-start | bytes 1048576 | tf_op jit(solution)/shard_map/psum | solution.py:189
  122.7 18.7 %all-to-all-start.2 = ((bf16[64,16,256]{2,0,1:T(8,128)(2,1)}), bf16[64,16,256]{2,0,1:T(8,128)(2,1)S(1)}, u32[]{:S(2)}, u32[]{:S(2)}) async-start(bf16[64,16,256]{2,0,1:T(8,128)(2,1)} %copy.119), calls=%async_computation.2 | async-start | bytes 1048576 | tf_op jit(solution)/shard_map/all_to_all | solution.py:223
  126.2 103.0 %all-gather.10.cloned.1.call-start = ((), (), s32[]{:S(2)}) async-start(), calls=%async_computation.18 | async-start | bytes 2621440 | tf_op jit(solution)/shard_map/all_gather | solution.py:227
  141.4 17.9 %all-to-all-start.3 = ((bf16[64,16,256]{2,0,1:T(8,128)(2,1)}), bf16[64,16,256]{2,0,1:T(8,128)(2,1)S(1)}, u32[]{:S(2)}, u32[]{:S(2)}) async-start(bf16[64,16,256]{2,0,1:T(8,128)(2,1)} %copy.122), calls=%async_computation.3 | async-start | bytes 1048576 | tf_op jit(solution)/shard_map/all_to_all | solution.py:224
  160.2 62.6 %all-to-all-start.5 = ((bf16[16,80,1024]{2,1,0:T(8,128)(2,1)}), bf16[16,80,1024]{2,1,0:T(8,128)(2,1)S(1)}, u32[]{:S(2)}, u32[]{:S(2)}) async-start(bf16[16,80,1024]{2,1,0:T(8,128)(2,1)} %bitcast.338), calls=%async_computation.5 | async-start | bytes 5242880 | tf_op jit(solution)/shard_map/all_to_all | solution.py:236
  163.8 68.6 %all-gather.12.cloned.1.call-start = ((), (), s32[]{:S(2)}) async-start(), calls=%async_computation.19 | async-start | bytes 2621440 | tf_op jit(solution)/shard_map/all_gather | solution.py:228
  222.7 63.5 %all-to-all-start = ((bf16[16,80,1024]{2,1,0:T(8,128)(2,1)}), bf16[16,80,1024]{2,1,0:T(8,128)(2,1)}, u32[]{:S(2)}, u32[]{:S(2)}) async-start(bf16[16,80,1024]{2,1,0:T(8,128)(2,1)} %bitcast.339), calls=%async_computation | async-start | bytes 5242880 | tf_op jit(solution)/shard_map/all_to_all | solution.py:235
  227.3 25.8 %all-gather.14.cloned.1.call-start = ((), (), s32[]{:S(2)}) async-start(), calls=%async_computation.20 | async-start | bytes 2621440 | tf_op jit(solution)/shard_map/all_gather | solution.py:229
  302.4 120.2 %all-to-all-start.6 = ((f32[4,320,1024]{2,0,1:T(4,128)}), f32[4,320,1024]{2,0,1:T(4,128)}, u32[]{:S(2)}, u32[]{:S(2)}) async-start(f32[4,320,1024]{2,0,1:T(4,128)} %copy.130), calls=%async_computation.6 | async-start | bytes 10485760 | tf_op jit(solution)/shard_map/all_to_all | solution.py:243
  307.5 163.2 %all-reduce.13.cloned.1.call-start = ((), (), s32[]{:S(2)}) async-start(), calls=%async_computation.21 | async-start | bytes 1048576 | tf_op jit(solution)/shard_map/psum | solution.py:267
  443.5 248.3 %reduce-scatter.8.cloned.1.call-start = ((), (), s32[]{:S(2)}) async-start(), calls=%async_computation.22 | async-start | bytes 655360 | tf_op jit(solution)/shard_map/reduce_scatter | solution.py:311
  483.0 211.9 %reduce-scatter.10.cloned.1.call-start = ((), (), s32[]{:S(2)}) async-start(), calls=%async_computation.23 | async-start | bytes 655360 | tf_op jit(solution)/shard_map/reduce_scatter | solution.py:312
  489.6 213.6 %reduce-scatter.20.cloned.1.call-start = ((), (), s32[]{:S(2)}) async-start(), calls=%async_computation.28 | async-start | bytes 15728640 | tf_op jit(solution)/shard_map/reduce_scatter | solution.py:255
  548.7 121.1 %all-to-all-start.4 = ((f32[4,320,1024]{2,0,1:T(4,128)}), f32[4,320,1024]{2,0,1:T(4,128)}, u32[]{:S(2)}, u32[]{:S(2)}) async-start(f32[4,320,1024]{2,0,1:T(4,128)} %copy.125), calls=%async_computation.4 | async-start | bytes 10485760 | tf_op jit(solution)/shard_map/all_to_all | solution.py:242
  554.3 182.5 %all-reduce.15.cloned.1.call-start = ((), (), s32[]{:S(2)}) async-start(), calls=%async_computation.29 | async-start | bytes 2097152 | tf_op jit(solution)/shard_map/psum | solution.py:267
  698.5 109.2 %reduce-scatter.14.cloned.1.call-start = ((), (), s32[]{:S(2)}) async-start(), calls=%async_computation.25 | async-start | bytes 1114112 | tf_op jit(solution)/shard_map/reduce_scatter | solution.py:345
  699.9 153.6 %reduce-scatter.16.cloned.1.call-start = ((), (), s32[]{:S(2)}) async-start(), calls=%async_computation.26 | async-start | bytes 1114112 | tf_op jit(solution)/shard_map/reduce_scatter | solution.py:346
  701.3 217.4 %reduce-scatter.12.cloned.1.call-start = ((), (), s32[]{:S(2)}) async-start(), calls=%async_computation.24 | async-start | bytes 2228224 | tf_op jit(solution)/shard_map/reduce_scatter | solution.py:344
  708.7 91.0 %all-to-all-start.7 = ((f32[256,3,4,256]{3,2,1,0:T(4,128)}), f32[256,3,4,256]{3,2,1,0:T(4,128)}, u32[]{:S(2)}, u32[]{:S(2)}) async-start(f32[256,3,4,256]{3,2,1,0:T(4,128)} %copy.141), calls=%async_computation.14 | async-start | bytes 6291456 | tf_op jit(solution)/shard_map/all_to_all | solution.py:256
  713.6 270.0 %reduce-scatter.18.cloned.1.call-start = ((), (), s32[]{:S(2)}) async-start(), calls=%async_computation.27 | async-start | bytes 2228224 | tf_op jit(solution)/shard_map/reduce_scatter | solution.py:347
  715.5 81.9 %copy-start.55 = (f32[128]{0:T(128)S(1)}, f32[128]{0:T(128)}, u32[]{:S(2)}) copy-start(f32[128]{0:T(128)} %get-tuple-element.263) | copy-start | bytes 1540
  (57 other events, 640.2 us)
Sparse Core Ops, SparseCore 0:
  11.1 44.2 all-gather.5
  57.5 38.5 all-gather.7
  121.8 26.1 all-reduce.10
  443.7 26.9 all-reduce.12
  698.6 38.0 all-reduce.14
Sparse Core Ops, SparseCore 1:
  128.9 23.1 all-gather.9
  166.5 23.1 all-gather.11
  229.9 23.1 all-gather.13
  483.1 21.5 reduce-scatter.7
  507.9 21.6 reduce-scatter.9
  538.9 98.9 reduce-scatter.19
  703.6 89.1 reduce-scatter.13
  796.9 56.6 reduce-scatter.15
  858.2 60.5 reduce-scatter.11
  923.1 60.5 reduce-scatter.17
where the time goes:
time: 1000 us; the launch traced here: 991 us
  waiting for transfers between devices  561 us (56%)
  blocking collectives  144 us (14%)
  local copies, waits for them, and re-layouts  133 us (13%)
  matrix products  48.6 us (5%)
  other arithmetic  47.7 us (5%)
  starting transfers between devices  38.4 us (4%)
  between operations  18 us (2%)
    all_to_all x1, waiting for transfers between devices, body(): lax.all_to_all(local_out, 'shard', split_axis=1, concat_axis=0, tiled=True)  115 us
    all_to_all x1, waiting for transfers between devices, body(): lax.all_to_all(local_grad, 'shard', split_axis=1, concat_axis=0, tiled=True)  115 us
    unnamed x2, blocking collectives  92.3 us
    reduce_scatter x1, waiting for transfers between devices, body(): lax.psum_scatter(term_query, ('shard', 'context'), scatter_dimension=0, t...  65.2 us
    reduce_scatter x1, waiting for transfers between devices, body(): lax.psum_scatter(term_output, ('shard', 'context'), scatter_dimension=0,...  64.9 us
    psum x2, waiting for transfers between devices, body(): moe, grad_normed_two = lax.psum((moe_part, normed_two_part), 'tensor')  47.6 us
    all_to_all x1, waiting for transfers between devices, body(): lax.all_to_all(grad_buffer, 'shard', split_axis=0, concat_axis=1, tiled=T...  46.5 us
    reduce_scatter x1, waiting for transfers between devices, body(): lax.psum_scatter(term_value, ('shard', 'context'), scatter_dimension=0, t...  45.9 us
  transfers between devices with their start and end apart: 23, of which 12 were waited for; matrix products, arithmetic and copies ran while one was open for 18% of the time, Pallas kernels for 0%

commit v1 on v0

v1 whole, which is shorter than its diff:
```python
import jax
import jax.numpy as jnp
from jax import lax
from jax.sharding import PartitionSpec as P

HEAD_DIM = 64


EPS = 1e-06
SCORE_SCALE = 0.015625
RESIDUAL_SCALE = 0.22
ROPE_BASE = 10000.0
NEG = -1e30


def rope_tables(positions, head_width):
    half_width = head_width // 2
    frequency = ROPE_BASE ** (-2.0 * jnp.arange(half_width, dtype=jnp.float32) / head_width)
    angles = positions.astype(jnp.float32)[:, None] * frequency[None, :]
    angles = jnp.concatenate([angles, angles], axis=1)
    return (jnp.cos(angles), jnp.sin(angles))


def apply_rotary(value_rows, cosine_table, rotary_sine_values):
    half_width = value_rows.shape[-1] // 2
    first_half = value_rows[..., :half_width]
    second_half = value_rows[..., half_width:]
    turned = jnp.concatenate([-second_half, first_half], axis=-1)
    return value_rows * cosine_table[:, None, :] + turned * rotary_sine_values[:, None, :]


def reverse_rotary(grads_in, cosine_table, rotary_sine_values):
    half_width = grads_in.shape[-1] // 2
    product = grads_in * rotary_sine_values[:, None, :]
    turned = jnp.concatenate([product[..., half_width:], -product[..., :half_width]], axis=-1)
    return grads_in * cosine_table[:, None, :] + turned


def inverse_rms(value_rows):
    return lax.rsqrt(jnp.mean(value_rows * value_rows, axis=-1, keepdims=True) + EPS)


def norm_backward(grad_normed, source, factor, gain_vector):
    scaled = grad_normed * gain_vector
    return factor * scaled - source * (factor * factor * factor) * jnp.mean(
        scaled * source, axis=-1, keepdims=True
    )


def contract_rows(left, right):
    return lax.dot_general(
        left, right, (((0,), (0,)), ((), ())), preferred_element_type=jnp.float32
    )


def contract_cols(left, right):
    return lax.dot_general(
        left, right, (((1,), (1,)), ((), ())), preferred_element_type=jnp.float32
    )


def exchange(array, axis, bit):
    size = lax.axis_size(axis)
    return lax.ppermute(array, axis, [(i, i ^ bit) for i in range(size)])


def pair_sum(part, axis):
    kept = lax.reduce_precision(part, 8, 7)
    return kept + exchange(kept.astype(jnp.bfloat16), axis, 1).astype(jnp.float32)


def axis_bits(axis):
    size = lax.axis_size(axis)
    bits = []
    bit = 1
    while bit < size:
        bits.append(bit)
        bit *= 2
    return bits


def halving_sum(terms, axis, dim):
    index = lax.axis_index(axis)
    for bit in axis_bits(axis):
        shape = terms.shape
        pairs = terms.reshape(shape[:dim] + (shape[dim] // 2, 2) + shape[dim + 1 :])
        mine = (index // bit) % 2
        low = lax.index_in_dim(pairs, 0, dim + 1, keepdims=False)
        high = lax.index_in_dim(pairs, 1, dim + 1, keepdims=False)
        sent = jnp.where(mine == 0, high, low).astype(jnp.bfloat16)
        kept = jnp.where(mine == 0, low, high)
        terms = kept.astype(jnp.float32) + exchange(sent, axis, bit).astype(jnp.float32)
    return lax.index_in_dim(terms, 0, dim, keepdims=False)


def relative_gather(block, axis):
    blocks = block[None]
    for bit in axis_bits(axis):
        blocks = jnp.concatenate([blocks, exchange(blocks, axis, bit)], axis=0)
    return blocks


def relative_sum(blocks, axis):
    for bit in reversed(axis_bits(axis)):
        received = exchange(blocks[bit:].astype(jnp.bfloat16), axis, bit)
        blocks = blocks[:bit] + received.astype(jnp.float32)
    return blocks[0]


def body(
    inputs,
    attn_gain,
    query_weight,
    key_weight,
    value_matrix,
    output_weight,
    ffn_gain,
    gate_weight,
    up_weight,
    down_weight,
    routes,
    route_weights,
    cotangent,
):
    f32, b16 = jnp.float32, jnp.bfloat16
    shard_count = lax.axis_size("shard")
    context_count = lax.axis_size("context")
    tokens = inputs[0]
    length, model_width = tokens.shape
    rows_own = query_weight.shape[0]
    q_cols, kv_cols = query_weight.shape[1], key_weight.shape[1]
    qkv_cols = q_cols + 2 * kv_cols
    kv_heads = kv_cols // HEAD_DIM
    heads = q_cols // HEAD_DIM
    group = heads // kv_heads
    experts, hidden_units = gate_weight.shape[1], gate_weight.shape[2]
    own_experts = experts // shard_count
    own_cols = own_experts * hidden_units

    gains = jnp.pad(jnp.stack([attn_gain, ffn_gain], axis=1), ((0, 0), (0, 126)))
    packed = jnp.concatenate(
        [query_weight, key_weight, value_matrix, output_weight, gains], axis=1
    )
    full = lax.all_gather(packed, ("shard", "context"), axis=0, tiled=True)
    qkv_full = full[:, :qkv_cols]
    output_full = full[:, qkv_cols : qkv_cols + q_cols]
    gain_rows = full[:, qkv_cols + q_cols :].astype(f32).T
    gain_attn, gain_ffn = gain_rows[0], gain_rows[1]

    grad_out = cotangent[0]
    expert_ids = jnp.arange(experts, dtype=jnp.int32)
    dense = jnp.sum(
        jnp.where(routes[0][:, :, None] == expert_ids, route_weights[0][:, :, None], 0.0), axis=1
    )
    dense_high = lax.reduce_precision(dense, 8, 7)
    dense_low = dense - dense_high
    early = jnp.concatenate(
        [
            grad_out.astype(b16),
            dense_high.astype(b16),
            dense_low.astype(b16),
            jnp.zeros((length, 128 - 2 * experts), b16),
        ],
        axis=1,
    )
    early_all = lax.all_gather(early, "shard", axis=0, tiled=True)

    stacked_weights = jnp.stack([gate_weight, up_weight, down_weight], axis=0)
    stacked_weights = stacked_weights.reshape(3, rows_own, shard_count, own_cols)
    stacked_weights = jnp.transpose(stacked_weights, (2, 0, 1, 3))
    owner = lax.all_to_all(stacked_weights, "shard", split_axis=0, concat_axis=0, tiled=True)
    expert_weights = lax.all_gather(owner, "context", axis=0, tiled=False)
    expert_weights = jnp.transpose(expert_weights, (2, 1, 0, 3, 4)).reshape(
        3, model_width, own_cols
    )
    own_gate, own_up, own_down = expert_weights[0], expert_weights[1], expert_weights[2]

    context_index = lax.axis_index("context")
    positions = context_index * length + jnp.arange(length, dtype=jnp.int32)
    cosine_table, rotary_sine_values = rope_tables(positions, HEAD_DIM)
    scale_one = inverse_rms(tokens)
    normed_one = (tokens * scale_one * gain_attn).astype(b16)
    qkv_lin = jnp.dot(normed_one, qkv_full, preferred_element_type=f32)
    turned = apply_rotary(
        qkv_lin[:, : q_cols + kv_cols].reshape(length, heads + kv_heads, HEAD_DIM),
        cosine_table,
        rotary_sine_values,
    ).astype(b16)
    query_rows = turned[:, :heads].reshape(length, kv_heads, group, HEAD_DIM)
    key_rows = turned[:, heads:].reshape(length, kv_cols)
    kv_rows = jnp.concatenate([key_rows, qkv_lin[:, q_cols + kv_cols :].astype(b16)], axis=1)
    kv_all = relative_gather(kv_rows, "context").reshape(context_count * length, 2 * kv_cols)
    keys = kv_all[:, :kv_cols].reshape(-1, kv_heads, HEAD_DIM)
    values = kv_all[:, kv_cols:].reshape(-1, kv_heads, HEAD_DIM)
    owners = context_index ^ jnp.arange(context_count, dtype=jnp.int32)
    key_pos = (
        owners[:, None] * length + jnp.arange(length, dtype=jnp.int32)[None, :]
    ).reshape(-1)
    visible = key_pos[None, :] <= positions[:, None]
    scores = (
        jnp.einsum("tkgd,skd->kgts", query_rows, keys, preferred_element_type=f32) * SCORE_SCALE
    )
    masked = jnp.where(visible, scores, NEG)
    weights_exp = jnp.where(visible, jnp.exp(masked - jnp.max(masked, -1, keepdims=True)), 0.0)
    soft = weights_exp / jnp.sum(weights_exp, axis=-1, keepdims=True)
    soft_b = soft.astype(b16)
    attended = jnp.einsum("kgts,skd->tkgd", soft_b, values, preferred_element_type=f32).astype(b16)
    attended_context = attended.reshape(length, q_cols)
    attn_out = pair_sum(contract_cols(attended_context, output_full), "tensor")
    hidden = tokens + RESIDUAL_SCALE * attn_out
    scale_two = inverse_rms(hidden)
    normed_two = (hidden * scale_two * gain_ffn).astype(b16)

    x_all = lax.all_gather(normed_two, "shard", axis=0, tiled=True)
    g_all = early_all[:, :model_width]
    dense_all = early_all[:, model_width : model_width + experts].astype(f32) + early_all[
        :, model_width + experts : model_width + 2 * experts
    ].astype(f32)
    dense_own = lax.dynamic_slice_in_dim(
        dense_all, lax.axis_index("shard") * own_experts, own_experts, 1
    )
    spread = jnp.repeat(dense_own, hidden_units, axis=1)
    grad_act = contract_dense(g_all, own_down) * (RESIDUAL_SCALE * spread)
    gate_act = contract_dense(x_all, own_gate)
    up_act = contract_dense(x_all, own_up)
    sigma = jax.nn.sigmoid(gate_act)
    swish = gate_act * sigma
    activated = (swish * up_act * spread).astype(b16)
    grad_gate = (grad_act * up_act * sigma * (1.0 + gate_act * (1.0 - sigma))).astype(b16)
    grad_up = (grad_act * swish).astype(b16)
    normed_two_terms = (contract_cols(grad_gate, own_gate) + contract_cols(grad_up, own_up)).astype(
        b16
    )
    normed_two_parts = lax.all_to_all(
        normed_two_terms.reshape(shard_count, length, model_width), "shard", 0, 0, tiled=True
    )
    moe_terms = contract_cols(activated, own_down).astype(b16)
    moe_parts = lax.all_to_all(
        moe_terms.reshape(shard_count, length, model_width), "shard", 0, 0, tiled=True
    )
    grad_normed_two = pair_sum(jnp.sum(normed_two_parts.astype(f32), axis=0), "tensor")
    moe = pair_sum(jnp.sum(moe_parts.astype(f32), axis=0), "tensor")
    output = hidden + RESIDUAL_SCALE * moe

    expert_terms = jnp.stack(
        [
            contract_rows(x_all, grad_gate),
            contract_rows(x_all, grad_up),
            RESIDUAL_SCALE * contract_rows(g_all, activated),
        ],
        axis=0,
    ).astype(b16)
    expert_terms = jnp.transpose(
        expert_terms.reshape(3, shard_count, context_count, rows_own, own_cols), (1, 2, 0, 3, 4)
    )
    context_sums = halving_sum(expert_terms, "context", 1).astype(b16)
    expert_sums = lax.all_to_all(context_sums, "shard", 0, 0, tiled=True)
    expert_sums = (
        jnp.transpose(expert_sums, (1, 2, 0, 3))
        .reshape(3, rows_own, experts, hidden_units)
        .astype(f32)
    )

    term_ffn_gain = jnp.sum(grad_normed_two * hidden * scale_two, axis=0)
    grad_hidden = grad_out + norm_backward(grad_normed_two, hidden, scale_two, gain_ffn)
    grad_attn = (RESIDUAL_SCALE * grad_hidden).astype(b16)
    context_gradient = jnp.dot(grad_attn, output_full, preferred_element_type=f32).astype(b16)
    grad_heads = context_gradient.reshape(length, kv_heads, group, HEAD_DIM)
    delta = jnp.transpose(
        jnp.sum(grad_heads.astype(f32) * attended.astype(f32), axis=-1), (1, 2, 0)
    )
    grad_soft = jnp.einsum("tkgd,skd->kgts", grad_heads, values, preferred_element_type=f32)
    grad_scores = (soft * (grad_soft - delta[..., None])).astype(b16)
    value_term = jnp.einsum("kgts,tkgd->skd", soft_b, grad_heads, preferred_element_type=f32)
    key_term = SCORE_SCALE * jnp.einsum(
        "kgts,tkgd->skd", grad_scores, query_rows, preferred_element_type=f32
    )
    kv_terms = jnp.concatenate(
        [key_term.reshape(-1, kv_cols), value_term.reshape(-1, kv_cols)], axis=1
    ).reshape(context_count, length, 2 * kv_cols)
    kv_sum = relative_sum(kv_terms, "context")
    grad_query = SCORE_SCALE * jnp.einsum(
        "kgts,skd->tkgd", grad_scores, keys, preferred_element_type=f32
    )
    term_output = contract_rows(grad_attn, attended_context)
    turned_back = reverse_rotary(
        jnp.concatenate(
            [
                grad_query.reshape(length, heads, HEAD_DIM),
                kv_sum[:, :kv_cols].reshape(length, kv_heads, HEAD_DIM),
            ],
            axis=1,
        ),
        cosine_table,
        rotary_sine_values,
    ).reshape(length, q_cols + kv_cols)
    grad_qkv = jnp.concatenate([turned_back, kv_sum[:, kv_cols:]], axis=1).astype(b16)
    term_qkv = contract_rows(normed_one, grad_qkv)
    normed_one_part = contract_cols(grad_qkv, qkv_full)
    term_attn_gain = jnp.sum(normed_one_part * tokens * scale_one, axis=0)
    gain_terms = jnp.pad(jnp.stack([term_attn_gain, term_ffn_gain], axis=0), ((0, 126), (0, 0))).T
    sum_output = scatter_rows(term_output, shard_count, context_count)
    sum_rest = scatter_rows(
        jnp.concatenate([term_qkv, gain_terms], axis=1), shard_count, context_count
    )
    grad_normed_one = pair_sum(normed_one_part, "tensor")
    grad_input = grad_hidden + norm_backward(grad_normed_one, tokens, scale_one, gain_attn)
    own_gains = sum_rest[:, qkv_cols:]
    sum_attn_gain = (own_gains + exchange(own_gains, "tensor", 1))[:, 0]
    return (
        output[None],
        grad_input[None],
        sum_attn_gain,
        sum_rest[:, :q_cols],
        sum_rest[:, q_cols : q_cols + kv_cols],
        sum_rest[:, q_cols + kv_cols : qkv_cols],
        sum_output,
        own_gains[:, 1],
        expert_sums[0],
        expert_sums[1],
        expert_sums[2],
    )


def contract_dense(left, right):
    return jnp.dot(left, right, preferred_element_type=jnp.float32)


def scatter_rows(term, shard_count, context_count):
    split = term.reshape(shard_count, context_count, -1, term.shape[1])
    return halving_sum(halving_sum(split, "context", 1), "shard", 0)


def solution(mesh):
    placed = (
        P("shard", "context", None),
        P(("shard", "context")),
        P(("shard", "context"), "tensor"),
        P(("shard", "context"), "tensor"),
        P(("shard", "context"), "tensor"),
        P(("shard", "context"), "tensor"),
        P(("shard", "context")),
        P(("shard", "context"), None, "tensor"),
        P(("shard", "context"), None, "tensor"),
        P(("shard", "context"), None, "tensor"),
        P("shard", "context", None),
        P("shard", "context", None),
        P("shard", "context", None),
    )
    return jax.shard_map(
        body,
        mesh=mesh,
        in_specs=placed,
        out_specs=(
            P("shard", "context", None),
            P("shard", "context", None),
            P(("shard", "context")),
            P(("shard", "context"), "tensor"),
            P(("shard", "context"), "tensor"),
            P(("shard", "context"), "tensor"),
            P(("shard", "context"), "tensor"),
            P(("shard", "context")),
            P(("shard", "context"), None, "tensor"),
            P(("shard", "context"), None, "tensor"),
            P(("shard", "context"), None, "tensor"),
        ),
        check_vma=False,
    )
```

time: 1000 us -> 449 us (0.45)
  waiting for transfers between devices: 561 us -> 260 us
  blocking collectives: 144 us -> 0 us
  local copies, waits for them, and re-layouts: 133 us -> 46.9 us
    all_to_all x8 -> x4, waiting for transfers between devices: 320 us -> 87.9 us  [the longest x1 55.5 us: body(): lax.all_to_all(stacked_weights, 'shard', split_axis=0, concat_axis=0, til...]
    reduce_scatter x7 -> x0, waiting for transfers between devices: 176 us -> none  [the longest x1 65.2 us: body(): lax.psum_scatter(term_query, ('shard', 'context'), scatter_dimension=0, t...]
    ppermute x0 -> x19, waiting for transfers between devices: none -> 110 us  [exchange(): return lax.ppermute(array, axis, [(i, i ^ bit) for i in range(size)])]
    unnamed x2 -> x0, blocking collectives: 92.3 us -> none
    all_gather x4 -> x0, blocking collectives: 51.7 us -> none  [the longest x1 20.5 us: body(): lax.all_gather(value_matrix, ('shard', 'context'), axis=0, tiled=True)]
    psum x3 -> x0, waiting for transfers between devices: 47.7 us -> none  [the longest x2 47.6 us: body(): moe, grad_normed_two = lax.psum((moe_part, normed_two_part), 'tensor')]
    all_gather x5 -> x4, waiting for transfers between devices: 15.7 us -> 61.8 us  [the longest x1 43.2 us: body(): expert_weights = lax.all_gather(owner, 'context', axis=0, tiled=False)]
    transpose x7 -> x1, local copies, waits for them, and re-layouts: 37.1 us -> 1.65 us  [body(): stacked_weights = jnp.transpose(stacked_weights, (2, 0, 1, 3))]
  transfers between devices with their start and end apart: 23 -> 27, of which waited for: 12 -> 16; matrix products, arithmetic and copies ran while one was open for 18% -> 22% of each run, Pallas kernels for 0% -> 0%
where the time goes in v1:
time: 449 us; the launch traced here: 444 us
  waiting for transfers between devices  260 us (58%)
  local copies, waits for them, and re-layouts  46.9 us (10%)
  other arithmetic  41.8 us (9%)
  matrix products  41.5 us (9%)
  starting transfers between devices  38.9 us (9%)
  between operations  15.4 us (3%)
    ppermute x19, waiting for transfers between devices, exchange(): return lax.ppermute(array, axis, [(i, i ^ bit) for i in range(size)])  110 us
    all_to_all x1, waiting for transfers between devices, body(): lax.all_to_all(stacked_weights, 'shard', split_axis=0, concat_axis=0, til...  55.5 us
    all_gather x1, waiting for transfers between devices, body(): expert_weights = lax.all_gather(owner, 'context', axis=0, tiled=False)  43.2 us
    ppermute x19, starting transfers between devices, exchange(): return lax.ppermute(array, axis, [(i, i ^ bit) for i in range(size)])  20 us
    all_to_all x1, waiting for transfers between devices, body(): lax.all_to_all(normed_two_terms.reshape(shard_count, length, model_width)...  19.2 us
    all_gather x1, waiting for transfers between devices, body(): x_all = lax.all_gather(normed_two, 'shard', axis=0, tiled=True)  18.6 us
    all_to_all x1, waiting for transfers between devices, body(): lax.all_to_all(moe_terms.reshape(shard_count, length, model_width), 'shar...  13.1 us
    unnamed x90, local copies, waits for them, and re-layouts  12.8 us
  transfers between devices with their start and end apart: 27, of which 16 were waited for; matrix products, arithmetic and copies ran while one was open for 22% of the time, Pallas kernels for 0%

profile of v1, /device:TPU:0, one launch (start us, length us, event | category | flops | bytes accessed | tf_op | source)
XLA Modules:
  0.0 444.4 jit_solution(15313373909633710738)
XLA Ops:
  17.7 6.4 %all-to-all-start = ((bf16[4,3,64,1024]{3,2,1,0:T(8,128)(2,1)}), bf16[4,3,64,1024]{3,2,1,0:T(8,128)(2,1)S(1)}, u32[]{:S(2)}, u32[]{:S(2)}) async-start(bf16[4,3,64,1024]{3,2,1,0:T(8,128)(2,1)} %copy.313), calls=%async_computation | async-start | bytes 3145728 | tf_op jit(solution)/shard_map/all_to_all | solution.py:171
  25.4 55.5 %all-to-all-done = bf16[4,3,64,1024]{3,2,1,0:T(8,128)(2,1)S(1)} async-done(((bf16[4,3,64,1024]{3,2,1,0:T(8,128)(2,1)}), bf16[4,3,64,1024]{3,2,1,0:T(8,128)(2,1)S(1)}, u32[]{:S(2)}, u32[]{:S(2)}) %all-to-all-start) | async-done | bytes 1572896 | tf_op jit(solution)/shard_map/all_to_all | solution.py:171
  90.5 6.7 %collective-permute-done.1 = bf16[2,128,512]{2,1,0:T(8,128)(2,1)S(1)} collective-permute-done((bf16[2,128,512]{2,1,0:T(8,128)(2,1)S(1)}, bf16[2,128,512]{2,1,0:T(8,128)(2,1)S(1)}, u32[]{:S(2)}, u32[]{:S(2)}) %collective-permute-start.1) | collective-permute-done | bytes 262176 | tf_op jit(solution)/shard_map/ppermute | solution.py:64
  105.2 6.2 %collective-permute-done.2 = bf16[128,1024]{1,0:T(8,128)(2,1)S(1)} collective-permute-done((bf16[128,1024]{1,0:T(8,128)(2,1)S(1)}, bf16[128,1024]{1,0:T(8,128)(2,1)S(1)}, u32[]{:S(2)}, u32[]{:S(2)}) %collective-permute-start.2) | collective-permute-done | bytes 262176 | tf_op jit(solution)/shard_map/ppermute | solution.py:64
  116.6 43.2 %all-gather.12.cloned.1.call-done = bf16[16,3,64,1024]{3,2,1,0:T(8,128)(2,1)} async-done(((bf16[4,3,64,1024]{3,2,1,0:T(8,128)(2,1)}), bf16[16,3,64,1024]{3,2,1,0:T(8,128)(2,1)}) %all-gather.12.cloned.1.call-update) | async-done | bytes 6291472 | tf_op jit(solution)/shard_map/all_gather | solution.py:172
  159.7 4.1 fusion.80
  171.1 18.6 %all-gather.8.cloned.1.call-done = bf16[512,1024]{1,0:T(8,128)(2,1)} async-done(((bf16[128,1024]{1,0:T(8,128)(2,1)}), bf16[512,1024]{1,0:T(8,128)(2,1)}) %all-gather.8.cloned.1.call-update) | async-done | bytes 1048592 | tf_op jit(solution)/shard_map/all_gather | solution.py:214
  189.7 3.3 fusion.88
  193.1 4.8 %multiply_convert_fusion.1 = (bf16[512,1024]{1,0:T(8,128)(2,1)S(1)}, bf16[512,1024]{1,0:T(8,128)(2,1)S(1)}, bf16[512,1024]{1,0:T(8,128)(2,1)}) fusion(f32[512,1024]{1,0:T(8,128)} %multiply_multiply_fusion, f32[512,1024]{1,0:T(8,128)S(1)} %fusion.88, f32[512,1024]{1,0:T(8,128)S(1)} %bitcast.373, bf16[512,1024]{1,0:T(8,128)(2,1)S(1)} %copy-done.35, ...), kind=kOutput, calls=%fused_computation.25 | convolution fusion | flops 1082130432 | bytes 12582912 | tf_op jit(solution)/shard_map/dot_general | solution.py:326
  202.8 4.3 all-to-all-start.2
  207.1 4.3 convolution_convert_fusion
  213.7 19.2 %all-to-all-done.2 = bf16[4,128,1024]{2,1,0:T(8,128)(2,1)} async-done(((bf16[4,128,1024]{2,1,0:T(8,128)(2,1)}), bf16[4,128,1024]{2,1,0:T(8,128)(2,1)}, u32[]{:S(2)}, u32[]{:S(2)}) %all-to-all-start.2) | async-done | bytes 1048608 | tf_op jit(solution)/shard_map/all_to_all | solution.py:234
  233.0 4.2 all-to-all-start.1
  237.3 3.0 convolution_convert_fusion.1
  249.4 13.1 %all-to-all-done.1 = bf16[4,128,1024]{2,1,0:T(8,128)(2,1)} async-done(((bf16[4,128,1024]{2,1,0:T(8,128)(2,1)}), bf16[4,128,1024]{2,1,0:T(8,128)(2,1)}, u32[]{:S(2)}, u32[]{:S(2)}) %all-to-all-start.1) | async-done | bytes 1048608 | tf_op jit(solution)/shard_map/all_to_all | solution.py:238
  266.4 5.0 %collective-permute-done.3 = bf16[128,1024]{1,0:T(8,128)(2,1)S(1)} collective-permute-done((bf16[128,1024]{1,0:T(8,128)(2,1)S(1)}, bf16[128,1024]{1,0:T(8,128)(2,1)S(1)}, u32[]{:S(2)}, u32[]{:S(2)}) %collective-permute-start.3) | collective-permute-done | bytes 262176 | tf_op jit(solution)/shard_map/ppermute | solution.py:64
  284.7 3.0 collective-permute-done.5
  308.0 6.4 %copy.327 = f32[1024,1152]{1,0:T(8,128)} copy(f32[1024,1152]{0,1:T(8,128)} %pad_maximum_fusion.1) | data formatting | bytes 9437184 | tf_op jit(solution)/shard_map/concatenate | solution.py:304
  317.5 6.2 %fusion.1 = f32[4,1,2,3,64,1024]{5,4,3,2,0,1:T(8,128)S(1)} fusion(bf16[4,2,3,64,1024]{4,3,2,1,0:T(8,128)(2,1)} %collective-permute-done.17, pred[]{:T(512)S(6)} %eq.61, bf16[4,2,2,3,64,1024]{5,4,3,2,1,0:T(8,128)(2,1)} %bitcast.354), kind=kLoop, calls=%fused_computation.3 | loop fusion | flops 6291456 | bytes 15728641 | tf_op jit(solution)/shard_map/reshape | solution.py:86
  327.7 12.7 %collective-permute-done.9 = bf16[4,1,64,1152]{3,2,0,1:T(8,128)(2,1)S(1)} collective-permute-done((bf16[4,1,64,1152]{3,2,0,1:T(8,128)(2,1)S(1)}, bf16[4,1,64,1152]{3,2,0,1:T(8,128)(2,1)S(1)}, u32[]{:S(2)}, u32[]{:S(2)}) %collective-permute-start.9) | collective-permute-done | bytes 589856 | tf_op jit(solution)/shard_map/ppermute | solution.py:64
  343.2 30.5 %collective-permute-done.18 = bf16[4,1,3,64,1024]{4,3,2,0,1:T(8,128)(2,1)S(1)} collective-permute-done((bf16[4,1,3,64,1024]{4,3,2,0,1:T(8,128)(2,1)S(1)}, bf16[4,1,3,64,1024]{4,3,2,0,1:T(8,128)(2,1)S(1)}, u32[]{:S(2)}, u32[]{:S(2)}) %collective-permute-start.18) | collective-permute-done | bytes 1572896 | tf_op jit(solution)/shard_map/ppermute | solution.py:64
  375.8 3.6 all-to-all-start.3
  379.4 2.9 collective-permute-start.16
  382.6 40.9 %collective-permute-done.16 = bf16[1,64,512]{2,1,0:T(8,128)(2,1)S(1)} collective-permute-done((bf16[1,64,512]{2,1,0:T(8,128)(2,1)S(1)}, bf16[1,64,512]{2,1,0:T(8,128)(2,1)S(1)}, u32[]{:S(2)}, u32[]{:S(2)}) %collective-permute-start.16) | collective-permute-done | bytes 65568 | tf_op jit(solution)/shard_map/ppermute | solution.py:64
  (260 shorter events, 121.0 us)
Async XLA Ops:
  7.2 76.0 %all-gather.6.cloned.1.call-start = ((), (), s32[]{:S(2)}) async-start(), calls=%async_computation.4 | async-start | bytes 3620864 | tf_op jit(solution)/shard_map/all_gather | solution.py:144
  17.7 63.2 %all-to-all-start = ((bf16[4,3,64,1024]{3,2,1,0:T(8,128)(2,1)}), bf16[4,3,64,1024]{3,2,1,0:T(8,128)(2,1)S(1)}, u32[]{:S(2)}, u32[]{:S(2)}) async-start(bf16[4,3,64,1024]{3,2,1,0:T(8,128)(2,1)} %copy.313), calls=%async_computation | async-start | bytes 3145728 | tf_op jit(solution)/shard_map/all_to_all | solution.py:171
  24.1 88.8 %all-gather.10.cloned.1.call-start = ((), (), s32[]{:S(2)}) async-start(), calls=%async_computation.6 | async-start | bytes 1474560 | tf_op jit(solution)/shard_map/all_gather | solution.py:166
  25.3 134.4 %all-gather.12.cloned.1.call-start = ((), (), s32[]{:S(2)}) async-start(), calls=%async_computation.7 | async-start | bytes 7864320 | tf_op jit(solution)/shard_map/all_gather | solution.py:172
  82.1 107.6 %all-gather.8.cloned.1.call-start = ((), (), s32[]{:S(2)}) async-start(), calls=%async_computation.5 | async-start | bytes 1310720 | tf_op jit(solution)/shard_map/all_gather | solution.py:214
  88.7 8.4 %collective-permute-start.1 = (bf16[2,128,512]{2,1,0:T(8,128)(2,1)S(1)}, bf16[2,128,512]{2,1,0:T(8,128)(2,1)S(1)}, u32[]{:S(2)}, u32[]{:S(2)}) collective-permute-start(bf16[2,128,512]{2,1,0:T(8,128)(2,1)S(1)} %pad_maximum_fusion.5), channel_id=1, source_target_pairs={{0,4},{2,6},{4,0},{6,2},{1,5},{3,7},{5,1},{7,3},{8,12},{10,14},{12... | collective-permute-start | bytes 786440 | tf_op jit(solution)/shard_map/ppermute | solution.py:64
  103.6 7.7 %collective-permute-start.2 = (bf16[128,1024]{1,0:T(8,128)(2,1)S(1)}, bf16[128,1024]{1,0:T(8,128)(2,1)S(1)}, u32[]{:S(2)}, u32[]{:S(2)}) collective-permute-start(bf16[128,1024]{1,0:T(8,128)(2,1)S(1)} %get-tuple-element.51), channel_id=1, source_target_pairs={{0,1},{1,0},{2,3},{3,2},{4,5},{5,4},{6,7},{7,6},{8,9},{9,8},{10,11... | collective-permute-start | bytes 786440 | tf_op jit(solution)/shard_map/ppermute | solution.py:64
  202.8 30.2 %all-to-all-start.2 = ((bf16[4,128,1024]{2,1,0:T(8,128)(2,1)}), bf16[4,128,1024]{2,1,0:T(8,128)(2,1)}, u32[]{:S(2)}, u32[]{:S(2)}) async-start(bf16[4,128,1024]{2,1,0:T(8,128)(2,1)} %bitcast.391), calls=%async_computation.2 | async-start | bytes 2097152 | tf_op jit(solution)/shard_map/all_to_all | solution.py:234
  233.0 29.6 %all-to-all-start.1 = ((bf16[4,128,1024]{2,1,0:T(8,128)(2,1)}), bf16[4,128,1024]{2,1,0:T(8,128)(2,1)}, u32[]{:S(2)}, u32[]{:S(2)}) async-start(bf16[4,128,1024]{2,1,0:T(8,128)(2,1)} %bitcast.392), calls=%async_computation.1 | async-start | bytes 2097152 | tf_op jit(solution)/shard_map/all_to_all | solution.py:238
  246.3 71.1 %collective-permute-start.17 = (bf16[4,2,3,64,1024]{4,3,2,1,0:T(8,128)(2,1)}, bf16[4,2,3,64,1024]{4,3,2,1,0:T(8,128)(2,1)}, u32[]{:S(2)}, u32[]{:S(2)}) collective-permute-start(bf16[4,2,3,64,1024]{4,3,2,1,0:T(8,128)(2,1)} %fusion.2), channel_id=1, source_target_pairs={{0,2},{2,0},{4,6},{6,4},{1,3},{3,1},{5,7},{7,5},{8,10},{10,8},{12,... | collective-permute-start | bytes 9437192 | tf_op jit(solution)/shard_map/ppermute | solution.py:64
  247.9 17.7 %collective-permute-start.4 = (bf16[128,1024]{1,0:T(8,128)(2,1)S(1)}, bf16[128,1024]{1,0:T(8,128)(2,1)S(1)}, u32[]{:S(2)}, u32[]{:S(2)}) collective-permute-start(bf16[128,1024]{1,0:T(8,128)(2,1)S(1)} %reduce-precision_convert_fusion.1), channel_id=1, source_target_pairs={{0,1},{1,0},{2,3},{3,2},{4,5},{5,4},{6,7},{7,6},{8,9},{9,8},{10,11... | collective-permute-start | bytes 786440 | tf_op jit(solution)/shard_map/ppermute | solution.py:64
  264.1 7.3 %collective-permute-start.3 = (bf16[128,1024]{1,0:T(8,128)(2,1)S(1)}, bf16[128,1024]{1,0:T(8,128)(2,1)S(1)}, u32[]{:S(2)}, u32[]{:S(2)}) collective-permute-start(bf16[128,1024]{1,0:T(8,128)(2,1)S(1)} %reduce-precision_convert_fusion.2), channel_id=1, source_target_pairs={{0,1},{1,0},{2,3},{3,2},{4,5},{5,4},{6,7},{7,6},{8,9},{9,8},{10,11... | collective-permute-start | bytes 786440 | tf_op jit(solution)/shard_map/ppermute | solution.py:64
  281.0 6.7 %collective-permute-start.5 = (bf16[2,128,512]{2,1,0:T(8,128)(2,1)}, bf16[2,128,512]{2,1,0:T(8,128)(2,1)}, u32[]{:S(2)}, u32[]{:S(2)}) collective-permute-start(bf16[2,128,512]{2,1,0:T(8,128)(2,1)} %bitcast.50), channel_id=1, source_target_pairs={{0,4},{2,6},{4,0},{6,2},{1,5},{3,7},{5,1},{7,3},{8,12},{10,14},{12... | collective-permute-start | bytes 786440 | tf_op jit(solution)/shard_map/ppermute | solution.py:64
  289.7 9.4 %collective-permute-start.13 = (bf16[4,2,64,512]{3,2,1,0:T(8,128)(2,1)}, bf16[4,2,64,512]{3,2,1,0:T(8,128)(2,1)}, u32[]{:S(2)}, u32[]{:S(2)}) collective-permute-start(bf16[4,2,64,512]{3,2,1,0:T(8,128)(2,1)} %fusion.35), channel_id=1, source_target_pairs={{0,2},{2,0},{4,6},{6,4},{1,3},{3,1},{5,7},{7,5},{8,10},{10,8},{12,... | collective-permute-start | bytes 1572872 | tf_op jit(solution)/shard_map/ppermute | solution.py:64
  296.8 8.4 %collective-permute-start.7 = (bf16[128,1024]{1,0:T(8,128)(2,1)S(1)}, bf16[128,1024]{1,0:T(8,128)(2,1)S(1)}, u32[]{:S(2)}, u32[]{:S(2)}) collective-permute-start(bf16[128,1024]{1,0:T(8,128)(2,1)S(1)} %get-tuple-element.53), channel_id=1, source_target_pairs={{0,1},{1,0},{2,3},{3,2},{4,5},{5,4},{6,7},{7,6},{8,9},{9,8},{10,11... | collective-permute-start | bytes 786440 | tf_op jit(solution)/shard_map/ppermute | solution.py:64
  301.5 15.7 %collective-permute-start.14 = (bf16[4,1,64,512]{3,2,0,1:T(8,128)(2,1)S(1)}, bf16[4,1,64,512]{3,2,0,1:T(8,128)(2,1)S(1)}, u32[]{:S(2)}, u32[]{:S(2)}) collective-permute-start(bf16[4,1,64,512]{3,2,0,1:T(8,128)(2,1)S(1)} %fusion.57), channel_id=1, source_target_pairs={{0,4},{2,6},{4,0},{6,2},{1,5},{3,7},{5,1},{7,3},{8,12},{10,14},{12... | collective-permute-start | bytes 786440 | tf_op jit(solution)/shard_map/ppermute | solution.py:64
  317.1 6.6 %collective-permute-start.8 = (bf16[4,2,64,1152]{3,2,1,0:T(8,128)(2,1)S(1)}, bf16[4,2,64,1152]{3,2,1,0:T(8,128)(2,1)S(1)}, u32[]{:S(2)}, u32[]{:S(2)}) collective-permute-start(bf16[4,2,64,1152]{3,2,1,0:T(8,128)(2,1)S(1)} %fusion.19), channel_id=1, source_target_pairs={{0,2},{2,0},{4,6},{6,4},{1,3},{3,1},{5,7},{7,5},{8,10},{10,8},{12,... | collective-permute-start | bytes 3538952 | tf_op jit(solution)/shard_map/ppermute | solution.py:64
  317.4 10.2 %collective-permute-start.15 = (bf16[2,64,512]{2,1,0:T(8,128)(2,1)S(1)}, bf16[2,64,512]{2,1,0:T(8,128)(2,1)S(1)}, u32[]{:S(2)}, u32[]{:S(2)}) collective-permute-start(bf16[2,64,512]{2,1,0:T(8,128)(2,1)S(1)} %fusion.64), channel_id=1, source_target_pairs={{0,8},{8,0},{16,24},{24,16},{1,9},{9,1},{17,25},{25,17},{2,10},{10... | collective-permute-start | bytes 393224 | tf_op jit(solution)/shard_map/ppermute | solution.py:64
  324.2 16.2 %collective-permute-start.9 = (bf16[4,1,64,1152]{3,2,0,1:T(8,128)(2,1)S(1)}, bf16[4,1,64,1152]{3,2,0,1:T(8,128)(2,1)S(1)}, u32[]{:S(2)}, u32[]{:S(2)}) collective-permute-start(bf16[4,1,64,1152]{3,2,0,1:T(8,128)(2,1)S(1)} %fusion.31), channel_id=1, source_target_pairs={{0,4},{2,6},{4,0},{6,2},{1,5},{3,7},{5,1},{7,3},{8,12},{10,14},{12... | collective-permute-start | bytes 1769480 | tf_op jit(solution)/shard_map/ppermute | solution.py:64
  326.0 47.7 %collective-permute-start.18 = (bf16[4,1,3,64,1024]{4,3,2,0,1:T(8,128)(2,1)S(1)}, bf16[4,1,3,64,1024]{4,3,2,0,1:T(8,128)(2,1)S(1)}, u32[]{:S(2)}, u32[]{:S(2)}) collective-permute-start(bf16[4,1,3,64,1024]{4,3,2,0,1:T(8,128)(2,1)S(1)} %fusion.16), channel_id=1, source_target_pairs={{0,4},{2,6},{4,0},{6,2},{1,5},{3,7},{5,1},{7,3},{8,12},{10,14},{12... | collective-permute-start | bytes 4718600 | tf_op jit(solution)/shard_map/ppermute | solution.py:64
  341.3 41.0 %collective-permute-start.10 = (bf16[2,64,1152]{2,1,0:T(8,128)(2,1)}, bf16[2,64,1152]{2,1,0:T(8,128)(2,1)S(1)}, u32[]{:S(2)}, u32[]{:S(2)}) collective-permute-start(bf16[2,64,1152]{2,1,0:T(8,128)(2,1)} %fusion.55), channel_id=1, source_target_pairs={{0,8},{8,0},{16,24},{24,16},{1,9},{9,1},{17,25},{25,17},{2,10},{10... | collective-permute-start | bytes 884744 | tf_op jit(solution)/shard_map/ppermute | solution.py:64
  375.8 54.4 %all-to-all-start.3 = ((bf16[4,3,64,1024]{3,2,1,0:T(8,128)(2,1)}), bf16[4,3,64,1024]{3,2,1,0:T(8,128)(2,1)S(1)}, u32[]{:S(2)}, u32[]{:S(2)}) async-start(bf16[4,3,64,1024]{3,2,1,0:T(8,128)(2,1)} %fusion.17), calls=%async_computation.3 | async-start | bytes 3145728 | tf_op jit(solution)/shard_map/all_to_all | solution.py:257
  379.4 44.0 %collective-permute-start.16 = (bf16[1,64,512]{2,1,0:T(8,128)(2,1)S(1)}, bf16[1,64,512]{2,1,0:T(8,128)(2,1)S(1)}, u32[]{:S(2)}, u32[]{:S(2)}) collective-permute-start(bf16[1,64,512]{2,1,0:T(8,128)(2,1)S(1)} %fusion.67), channel_id=1, source_target_pairs={{0,16},{8,24},{16,0},{24,8},{1,17},{9,25},{17,1},{25,9},{2,18},{10... | collective-permute-start | bytes 196616 | tf_op jit(solution)/shard_map/ppermute | solution.py:64
  382.5 43.1 %collective-permute-start.11 = (bf16[1,64,1152]{2,1,0:T(8,128)(2,1)S(1)}, bf16[1,64,1152]{2,1,0:T(8,128)(2,1)S(1)}, u32[]{:S(2)}, u32[]{:S(2)}) collective-permute-start(bf16[1,64,1152]{2,1,0:T(8,128)(2,1)S(1)} %fusion.63), channel_id=1, source_target_pairs={{0,16},{8,24},{16,0},{24,8},{1,17},{9,25},{17,1},{25,9},{2,18},{10... | collective-permute-start | bytes 442376 | tf_op jit(solution)/shard_map/ppermute | solution.py:64
  (45 other events, 214.0 us)
Sparse Core Ops, SparseCore 0:
  12.1 69.7 all-gather.5
  84.0 28.1 all-gather.9
  113.8 45.9 all-gather.11
  161.7 27.9 all-gather.7

commit v2 on v1

--- a/solution.py
+++ b/solution.py
@@ -79,31 +79,49 @@
     return bits
 
 
+def tie(*arrays):
+    return lax.optimization_barrier(arrays)
+
+
+def halving_step(terms, axis, dim, bit):
+    shape = terms.shape
+    pairs = terms.reshape(shape[:dim] + (shape[dim] // 2, 2) + shape[dim + 1 :])
+    mine = (lax.axis_index(axis) // bit) % 2
+    low = lax.index_in_dim(pairs, 0, dim + 1, keepdims=False)
+    high = lax.index_in_dim(pairs, 1, dim + 1, keepdims=False)
+    sent = jnp.where(mine == 0, high, low).astype(jnp.bfloat16)
+    kept = jnp.where(mine == 0, low, high)
+    return kept.astype(jnp.float32) + exchange(sent, axis, bit).astype(jnp.float32)
+
+
 def halving_sum(terms, axis, dim):
-    index = lax.axis_index(axis)
     for bit in axis_bits(axis):
-        shape = terms.shape
-        pairs = terms.reshape(shape[:dim] + (shape[dim] // 2, 2) + shape[dim + 1 :])
-        mine = (index // bit) % 2
-        low = lax.index_in_dim(pairs, 0, dim + 1, keepdims=False)
-        high = lax.index_in_dim(pairs, 1, dim + 1, keepdims=False)
-        sent = jnp.where(mine == 0, high, low).astype(jnp.bfloat16)
-        kept = jnp.where(mine == 0, low, high)
-        terms = kept.astype(jnp.float32) + exchange(sent, axis, bit).astype(jnp.float32)
+        terms = halving_step(terms, axis, dim, bit)
     return lax.index_in_dim(terms, 0, dim, keepdims=False)
+
+
+def ordered_step(blocks, axis, bit):
+    received = exchange(blocks, axis, bit)
+    mine = (lax.axis_index(axis) // bit) % 2
+    low = jnp.where(mine == 0, blocks, received)
+    high = jnp.where(mine == 0, received, blocks)
+    return jnp.stack([low, high], axis=1).reshape((-1,) + blocks.shape[1:])
 
 
 def relative_gather(block, axis):
     blocks = block[None]
+    offsets = [0]
+    for bit in reversed(axis_bits(axis)):
+        blocks = jnp.concatenate([blocks, exchange(blocks, axis, bit)], axis=0)
+        offsets = offsets + [offset ^ bit for offset in offsets]
+    return blocks, offsets
+
+
+def relative_sum(blocks, axis):
     for bit in axis_bits(axis):
-        blocks = jnp.concatenate([blocks, exchange(blocks, axis, bit)], axis=0)
-    return blocks
-
-
-def relative_sum(blocks, axis):
-    for bit in reversed(axis_bits(axis)):
-        received = exchange(blocks[bit:].astype(jnp.bfloat16), axis, bit)
-        blocks = blocks[:bit] + received.astype(jnp.float32)
+        half = blocks.shape[0] // 2
+        received = exchange(blocks[half:].astype(jnp.bfloat16), axis, bit)
+        blocks = blocks[:half] + received.astype(jnp.float32)
     return blocks[0]
 
 
@@ -141,11 +159,7 @@
     packed = jnp.concatenate(
         [query_weight, key_weight, value_matrix, output_weight, gains], axis=1
     )
-    full = lax.all_gather(packed, ("shard", "context"), axis=0, tiled=True)
-    qkv_full = full[:, :qkv_cols]
-    output_full = full[:, qkv_cols : qkv_cols + q_cols]
-    gain_rows = full[:, qkv_cols + q_cols :].astype(f32).T
-    gain_attn, gain_ffn = gain_rows[0], gain_rows[1]
+    packed_all = lax.all_gather(packed, "shard", axis=0, tiled=False)
 
     grad_out = cotangent[0]
     expert_ids = jnp.arange(experts, dtype=jnp.int32)
@@ -163,17 +177,27 @@
         ],
         axis=1,
     )
+    packed_all, early = tie(packed_all, early)
     early_all = lax.all_gather(early, "shard", axis=0, tiled=True)
+
+    bits = axis_bits("context")
+    full = packed_all[None]
+    for bit in reversed(bits):
+        full = ordered_step(full, "context", bit)
+    full = jnp.swapaxes(full, 0, 1).reshape(model_width, packed.shape[1])
+    qkv_full = full[:, :qkv_cols]
+    output_full = full[:, qkv_cols : qkv_cols + q_cols]
+    gain_rows = full[:, qkv_cols + q_cols :].astype(f32).T
+    gain_attn, gain_ffn = gain_rows[0], gain_rows[1]
 
     stacked_weights = jnp.stack([gate_weight, up_weight, down_weight], axis=0)
     stacked_weights = stacked_weights.reshape(3, rows_own, shard_count, own_cols)
     stacked_weights = jnp.transpose(stacked_weights, (2, 0, 1, 3))
     owner = lax.all_to_all(stacked_weights, "shard", split_axis=0, concat_axis=0, tiled=True)
-    expert_weights = lax.all_gather(owner, "context", axis=0, tiled=False)
-    expert_weights = jnp.transpose(expert_weights, (2, 1, 0, 3, 4)).reshape(
-        3, model_width, own_cols
-    )
-    own_gate, own_up, own_down = expert_weights[0], expert_weights[1], expert_weights[2]
+    qkv_full, owner = tie(qkv_full, owner)
+    expert_blocks = owner[None]
+    for bit in reversed(bits[1:]):
+        expert_blocks = ordered_step(expert_blocks, "context", bit)
 
     context_index = lax.axis_index("context")
     positions = context_index * length + jnp.arange(length, dtype=jnp.int32)
@@ -189,10 +213,11 @@
     query_rows = turned[:, :heads].reshape(length, kv_heads, group, HEAD_DIM)
     key_rows = turned[:, heads:].reshape(length, kv_cols)
     kv_rows = jnp.concatenate([key_rows, qkv_lin[:, q_cols + kv_cols :].astype(b16)], axis=1)
-    kv_all = relative_gather(kv_rows, "context").reshape(context_count * length, 2 * kv_cols)
+    kv_blocks, offsets = relative_gather(kv_rows, "context")
+    kv_all = kv_blocks.reshape(context_count * length, 2 * kv_cols)
     keys = kv_all[:, :kv_cols].reshape(-1, kv_heads, HEAD_DIM)
     values = kv_all[:, kv_cols:].reshape(-1, kv_heads, HEAD_DIM)
-    owners = context_index ^ jnp.arange(context_count, dtype=jnp.int32)
+    owners = context_index ^ jnp.array(offsets, dtype=jnp.int32)
     key_pos = (
         owners[:, None] * length + jnp.arange(length, dtype=jnp.int32)[None, :]
     ).reshape(-1)
@@ -211,6 +236,12 @@
     scale_two = inverse_rms(hidden)
     normed_two = (hidden * scale_two * gain_ffn).astype(b16)
 
+    normed_two, expert_blocks = tie(normed_two, expert_blocks)
+    expert_blocks = ordered_step(expert_blocks, "context", 1)
+    expert_weights = jnp.transpose(expert_blocks, (2, 1, 0, 3, 4)).reshape(
+        3, model_width, own_cols
+    )
+    own_gate, own_up, own_down = expert_weights[0], expert_weights[1], expert_weights[2]
     x_all = lax.all_gather(normed_two, "shard", axis=0, tiled=True)
     g_all = early_all[:, :model_width]
     dense_all = early_all[:, model_width : model_width + experts].astype(f32) + early_all[
@@ -239,8 +270,6 @@
         moe_terms.reshape(shard_count, length, model_width), "shard", 0, 0, tiled=True
     )
     grad_normed_two = pair_sum(jnp.sum(normed_two_parts.astype(f32), axis=0), "tensor")
-    moe = pair_sum(jnp.sum(moe_parts.astype(f32), axis=0), "tensor")
-    output = hidden + RESIDUAL_SCALE * moe
 
     expert_terms = jnp.stack(
         [
@@ -253,32 +282,39 @@
     expert_terms = jnp.transpose(
         expert_terms.reshape(3, shard_count, context_count, rows_own, own_cols), (1, 2, 0, 3, 4)
     )
-    context_sums = halving_sum(expert_terms, "context", 1).astype(b16)
+    expert_terms = halving_step(expert_terms, "context", 1, 1)
+
+    term_ffn_gain = jnp.sum(grad_normed_two * hidden * scale_two, axis=0)
+    grad_hidden = grad_out + norm_backward(grad_normed_two, hidden, scale_two, gain_ffn)
+    grad_attn = (RESIDUAL_SCALE * grad_hidden).astype(b16)
+    grad_attn, expert_terms = tie(grad_attn, expert_terms)
+    for bit in bits[1:]:
+        expert_terms = halving_step(expert_terms, "context", 1, bit)
+    context_sums = expert_terms[:, 0].astype(b16)
+    context_gradient = jnp.dot(grad_attn, output_full, preferred_element_type=f32).astype(b16)
+    grad_heads = context_gradient.reshape(length, kv_heads, group, HEAD_DIM)
+    delta = jnp.transpose(
+        jnp.sum(grad_heads.astype(f32) * attended.astype(f32), axis=-1), (1, 2, 0)
+    )
+    grad_soft = jnp.einsum("tkgd,skd->kgts", grad_heads, values, preferred_element_type=f32)
+    grad_scores = (soft * (grad_soft - delta[..., None])).astype(b16)
+    value_term = jnp.einsum("kgts,tkgd->skd", soft_b, grad_heads, preferred_element_type=f32)
+    key_term = SCORE_SCALE * jnp.einsum(
+        "kgts,tkgd->skd", grad_scores, query_rows, preferred_element_type=f32
+    )
+    kv_terms = jnp.concatenate(
+        [key_term.reshape(-1, kv_cols), value_term.reshape(-1, kv_cols)], axis=1
+    ).reshape(context_count, length, 2 * kv_cols)
+    kv_sum = relative_sum(kv_terms, "context")
+    kv_sum, moe_parts, context_sums = tie(kv_sum, moe_parts, context_sums)
+    moe = pair_sum(jnp.sum(moe_parts.astype(f32), axis=0), "tensor")
+    output = hidden + RESIDUAL_SCALE * moe
     expert_sums = lax.all_to_all(context_sums, "shard", 0, 0, tiled=True)
     expert_sums = (
         jnp.transpose(expert_sums, (1, 2, 0, 3))
         .reshape(3, rows_own, experts, hidden_units)
         .astype(f32)
     )
-
-    term_ffn_gain = jnp.sum(grad_normed_two * hidden * scale_two, axis=0)
-    grad_hidden = grad_out + norm_backward(grad_normed_two, hidden, scale_two, gain_ffn)
-    grad_attn = (RESIDUAL_SCALE * grad_hidden).astype(b16)
-    context_gradient = jnp.dot(grad_attn, output_full, preferred_element_type=f32).astype(b16)
-    grad_heads = context_gradient.reshape(length, kv_heads, group, HEAD_DIM)
-    delta = jnp.transpose(
-        jnp.sum(grad_heads.astype(f32) * attended.astype(f32), axis=-1), (1, 2, 0)
-    )
-    grad_soft = jnp.einsum("tkgd,skd->kgts", grad_heads, values, preferred_element_type=f32)
-    grad_scores = (soft * (grad_soft - delta[..., None])).astype(b16)
-    value_term = jnp.einsum("kgts,tkgd->skd", soft_b, grad_heads, preferred_element_type=f32)
-    key_term = SCORE_SCALE * jnp.einsum(
-        "kgts,tkgd->skd", grad_scores, query_rows, preferred_element_type=f32
-    )
-    kv_terms = jnp.concatenate(
-        [key_term.reshape(-1, kv_cols), value_term.reshape(-1, kv_cols)], axis=1
-    ).reshape(context_count, length, 2 * kv_cols)
-    kv_sum = relative_sum(kv_terms, "context")
     grad_query = SCORE_SCALE * jnp.einsum(
         "kgts,skd->tkgd", grad_scores, keys, preferred_element_type=f32
     )
@@ -298,15 +334,15 @@
     term_qkv = contract_rows(normed_one, grad_qkv)
     normed_one_part = contract_cols(grad_qkv, qkv_full)
     term_attn_gain = jnp.sum(normed_one_part * tokens * scale_one, axis=0)
-    gain_terms = jnp.pad(jnp.stack([term_attn_gain, term_ffn_gain], axis=0), ((0, 126), (0, 0))).T
+    gain_terms = jnp.concatenate(
+        [term_attn_gain.reshape(-1, rows_own), term_ffn_gain.reshape(-1, rows_own)], axis=1
+    )
     sum_output = scatter_rows(term_output, shard_count, context_count)
-    sum_rest = scatter_rows(
-        jnp.concatenate([term_qkv, gain_terms], axis=1), shard_count, context_count
-    )
+    sum_rest = scatter_rows(term_qkv, shard_count, context_count)
+    own_gains = scatter_rows(gain_terms, shard_count, context_count)
     grad_normed_one = pair_sum(normed_one_part, "tensor")
     grad_input = grad_hidden + norm_backward(grad_normed_one, tokens, scale_one, gain_attn)
-    own_gains = sum_rest[:, qkv_cols:]
-    sum_attn_gain = (own_gains + exchange(own_gains, "tensor", 1))[:, 0]
+    sum_attn_gain = (own_gains + exchange(own_gains, "tensor", 1))[0, :rows_own]
     return (
         output[None],
         grad_input[None],
@@ -315,7 +351,7 @@
         sum_rest[:, q_cols : q_cols + kv_cols],
         sum_rest[:, q_cols + kv_cols : qkv_cols],
         sum_output,
-        own_gains[:, 1],
+        own_gains[0, rows_own:],
         expert_sums[0],
         expert_sums[1],
         expert_sums[2],

time: 449 us -> 459 us (1.022)
  waiting for transfers between devices: 260 us -> 213 us
  other arithmetic: 41.8 us -> 65.5 us
  blocking collectives: 0 us -> 22.1 us
  starting transfers between devices: 38.9 us -> 50.7 us
  matrix products: 41.5 us -> 36.8 us
    all_gather x2 -> x0, waiting for transfers between devices: 43.2 us -> none  [the longest x1 43.2 us: body(): expert_weights = lax.all_gather(owner, 'context', axis=0, tiled=False)]
    all_gather x1, waiting for transfers between devices: 0.02 us -> 29.1 us  [body(): early_all = lax.all_gather(early, 'shard', axis=0, tiled=True)]
    all_to_all x1, waiting for transfers between devices: 55.5 us -> 32.2 us  [body(): lax.all_to_all(stacked_weights, 'shard', split_axis=0, concat_axis=0, til...]
    all_gather x0 -> x1, blocking collectives: none -> 22.1 us  [body(): packed_all = lax.all_gather(packed, 'shard', axis=0, tiled=False)]
    all_to_all x1, waiting for transfers between devices: 13.1 us -> 0.01 us  [body(): lax.all_to_all(moe_terms.reshape(shard_count, length, model_width), 'shar...]
    ppermute x19 -> x27, starting transfers between devices: 20 us -> 31 us  [exchange(): return lax.ppermute(array, axis, [(i, i ^ bit) for i in range(size)])]
    another operation x2 -> x8, other arithmetic: 1.54 us -> 11.9 us  [the longest x6 9.37 us: ordered_step(): return jnp.stack([low, high], axis=1).reshape((-1,) + blocks.shape[1:])]
    add x3 -> x6, other arithmetic: 1.31 us -> 9.3 us  [the longest x4 9.23 us: halving_step(): kept.astype(jnp.float32) + exchange(sent, axis, bit).astype(jnp.float32)]
  transfers between devices with their start and end apart: 27 -> 33, of which waited for: 16 -> 18; matrix products, arithmetic and copies ran while one was open for 22% -> 21% of each run, Pallas kernels for 0% -> 0%
where the time goes in v2:
time: 459 us; the launch traced here: 451 us
  waiting for transfers between devices  213 us (46%)
  other arithmetic  65.5 us (14%)
  starting transfers between devices  50.7 us (11%)
  local copies, waits for them, and re-layouts  47.1 us (10%)
  matrix products  36.8 us (8%)
  blocking collectives  22.1 us (5%)
  between operations  15.6 us (3%)
    ppermute x27, waiting for transfers between devices, exchange(): return lax.ppermute(array, axis, [(i, i ^ bit) for i in range(size)])  108 us
    all_to_all x1, waiting for transfers between devices, body(): lax.all_to_all(stacked_weights, 'shard', split_axis=0, concat_axis=0, til...  32.2 us
    ppermute x27, starting transfers between devices, exchange(): return lax.ppermute(array, axis, [(i, i ^ bit) for i in range(size)])  31 us
    all_gather x1, waiting for transfers between devices, body(): early_all = lax.all_gather(early, 'shard', axis=0, tiled=True)  29.1 us
    all_to_all x1, waiting for transfers between devices, body(): lax.all_to_all(normed_two_terms.reshape(shard_count, length, model_width)...  26.7 us
    all_gather x1, blocking collectives, body(): packed_all = lax.all_gather(packed, 'shard', axis=0, tiled=False)  22.1 us
    all_gather x1, waiting for transfers between devices, body(): x_all = lax.all_gather(normed_two, 'shard', axis=0, tiled=True)  16.2 us
    dot_general x5, matrix products, contract_cols(): lax.dot_general(left, right, (((1,), (1,)), ((), ())), preferred_element_...  12.7 us
  transfers between devices with their start and end apart: 33, of which 18 were waited for; matrix products, arithmetic and copies ran while one was open for 21% of the time, Pallas kernels for 0%

profile of v2, /device:TPU:0, one launch (start us, length us, event | category | flops | bytes accessed | tf_op | source)
XLA Modules:
  0.0 450.7 jit_solution(7917721871587269739)
XLA Ops:
  13.3 22.1 %all-gather = bf16[256,1664]{1,0:T(8,128)(2,1)S(1)} all-gather(bf16[64,1664]{1,0:T(8,128)(2,1)S(1)} %pad_dynamic-update-slice_fusion), channel_id=2, replica_groups=mesh['shard'=4,'context'=4,'tensor'=2] {'shard'}, dimensions={0}, use_global_device_ids=true | all-gather | bytes 1064960 | tf_op jit(solution)/shard_map/all_gather | solution.py:162
  37.7 16.5 %collective-permute-done = bf16[1,4,64,1664]{3,2,1,0:T(8,128)(2,1)} collective-permute-done((bf16[1,4,64,1664]{3,2,1,0:T(8,128)(2,1)S(1)}, bf16[1,4,64,1664]{3,2,1,0:T(8,128)(2,1)}, u32[]{:S(2)}, u32[]{:S(2)}) %collective-permute-start) | collective-permute-done | bytes 852000 | tf_op jit(solution)/shard_map/ppermute | solution.py:64
  64.4 4.8 %all-to-all-start = ((bf16[4,3,64,1024]{3,2,1,0:T(8,128)(2,1)}), bf16[4,3,64,1024]{3,2,1,0:T(8,128)(2,1)}, u32[]{:S(2)}, u32[]{:S(2)}) async-start(bf16[4,3,64,1024]{3,2,1,0:T(8,128)(2,1)} %copy.340), calls=%async_computation | async-start | bytes 3145728 | tf_op jit(solution)/shard_map/all_to_all | solution.py:196
  74.8 32.2 %all-to-all-done = bf16[4,3,64,1024]{3,2,1,0:T(8,128)(2,1)} async-done(((bf16[4,3,64,1024]{3,2,1,0:T(8,128)(2,1)}), bf16[4,3,64,1024]{3,2,1,0:T(8,128)(2,1)}, u32[]{:S(2)}, u32[]{:S(2)}) %all-to-all-start) | async-done | bytes 1572896 | tf_op jit(solution)/shard_map/all_to_all | solution.py:196
  109.5 3.5 collective-permute-done.2
  115.8 3.3 fusion.92
  127.0 6.9 %collective-permute-done.4 = bf16[128,1024]{1,0:T(8,128)(2,1)S(1)} collective-permute-done((bf16[128,1024]{1,0:T(8,128)(2,1)S(1)}, bf16[128,1024]{1,0:T(8,128)(2,1)S(1)}, u32[]{:S(2)}, u32[]{:S(2)}) %collective-permute-start.4) | collective-permute-done | bytes 262176 | tf_op jit(solution)/shard_map/ppermute | solution.py:64
  135.4 15.8 %collective-permute-done.5 = bf16[1,4,3,64,1024]{4,3,2,1,0:T(8,128)(2,1)} collective-permute-done((bf16[1,4,3,64,1024]{4,3,2,1,0:T(8,128)(2,1)}, bf16[1,4,3,64,1024]{4,3,2,1,0:T(8,128)(2,1)}, u32[]{:S(2)}, u32[]{:S(2)}) %collective-permute-start.5) | collective-permute-done | bytes 1572896 | tf_op jit(solution)/shard_map/ppermute | solution.py:64
  155.9 29.1 %all-gather.4.cloned.1.call-done = bf16[512,1152]{1,0:T(8,128)(2,1)} async-done(((bf16[128,1152]{1,0:T(8,128)(2,1)}), bf16[512,1152]{1,0:T(8,128)(2,1)}) %all-gather.4.cloned.1.call-update) | async-done | bytes 1179664 | tf_op jit(solution)/shard_map/all_gather | solution.py:181
  188.8 3.3 select_bitcast_fusion.1
  198.0 16.2 %all-gather.6.cloned.1.call-done = bf16[512,1024]{1,0:T(8,128)(2,1)} async-done(((bf16[128,1024]{1,0:T(8,128)(2,1)}), bf16[512,1024]{1,0:T(8,128)(2,1)}) %all-gather.6.cloned.1.call-update) | async-done | bytes 1048592 | tf_op jit(solution)/shard_map/all_gather | solution.py:245
  214.3 3.3 fusion.94
  235.7 4.3 all-to-all-start.1
  240.0 26.7 %all-to-all-done.1 = bf16[4,128,1024]{2,1,0:T(8,128)(2,1)} async-done(((bf16[4,128,1024]{2,1,0:T(8,128)(2,1)}), bf16[4,128,1024]{2,1,0:T(8,128)(2,1)}, u32[]{:S(2)}, u32[]{:S(2)}) %all-to-all-start.1) | async-done | bytes 1048608 | tf_op jit(solution)/shard_map/all_to_all | solution.py:265
  271.3 3.5 convolution_convert_fusion.2
  274.8 4.3 all-to-all-start.2
  284.6 8.8 %convert_add_fusion = f32[4,2,3,64,1024]{4,3,2,1,0:T(8,128)} fusion(bf16[4,2,3,64,1024]{4,3,2,1,0:T(8,128)(2,1)} %collective-permute-done.8, pred[]{:T(512)S(6)} %eq.35, bf16[4,2,2,3,64,1024]{5,4,3,2,1,0:T(8,128)(2,1)} %bitcast.462), kind=kLoop, calls=%fused_computation.3 | loop fusion | flops 6291456 | bytes 15728641 | tf_op jit(solution)/shard_map/add | solution.py:94
  310.2 3.3 fusion.13
  318.0 37.5 %collective-permute-done.24 = bf16[4,1,64,512]{3,2,0,1:T(8,128)(2,1)S(1)} collective-permute-done((bf16[4,1,64,512]{3,2,0,1:T(8,128)(2,1)S(1)}, bf16[4,1,64,512]{3,2,0,1:T(8,128)(2,1)S(1)}, u32[]{:S(2)}, u32[]{:S(2)}) %collective-permute-start.24) | collective-permute-done | bytes 262176 | tf_op jit(solution)/shard_map/ppermute | solution.py:64
  381.0 6.1 %all-to-all-start.3 = ((bf16[4,3,64,1024]{3,2,1,0:T(8,128)(2,1)}), bf16[4,3,64,1024]{3,2,1,0:T(8,128)(2,1)}, u32[]{:S(2)}, u32[]{:S(2)}) async-start(bf16[4,3,64,1024]{3,2,1,0:T(8,128)(2,1)} %fusion.14), calls=%async_computation.3 | async-start | bytes 3145728 | tf_op jit(solution)/shard_map/all_to_all | solution.py:312
  404.4 5.0 %collective-permute-done.16 = bf16[2,1,128]{2,0,1:T(2,128)(2,1)S(1)} collective-permute-done((bf16[2,1,128]{2,0,1:T(2,128)(2,1)S(1)}, bf16[2,1,128]{2,0,1:T(2,128)(2,1)S(1)}, u32[]{:S(2)}, u32[]{:S(2)}) %collective-permute-start.16) | collective-permute-done | bytes 544 | tf_op jit(solution)/shard_map/ppermute | solution.py:64
  409.4 4.6 %collective-permute-start.17 = (bf16[1,1,128]{2,1,0:T(2,128)(2,1)S(1)}, bf16[1,1,128]{2,1,0:T(2,128)(2,1)S(1)}, u32[]{:S(2)}, u32[]{:S(2)}) collective-permute-start(bf16[1,1,128]{2,1,0:T(2,128)(2,1)S(1)} %fusion.76), channel_id=1, source_target_pairs={{0,16},{8,24},{16,0},{24,8},{1,17},{9,25},{17,1},{25,9},{2,18},{10... | collective-permute-start | bytes 776 | tf_op jit(solution)/shard_map/ppermute | solution.py:64
  414.4 6.6 %collective-permute-done.17 = bf16[1,1,128]{2,1,0:T(2,128)(2,1)S(1)} collective-permute-done((bf16[1,1,128]{2,1,0:T(2,128)(2,1)S(1)}, bf16[1,1,128]{2,1,0:T(2,128)(2,1)S(1)}, u32[]{:S(2)}, u32[]{:S(2)}) %collective-permute-start.17) | collective-permute-done | bytes 288 | tf_op jit(solution)/shard_map/ppermute | solution.py:64
  426.6 6.9 %collective-permute-done.22 = bf16[1,64,1024]{2,1,0:T(8,128)(2,1)S(1)} collective-permute-done((bf16[1,64,1024]{2,1,0:T(8,128)(2,1)S(1)}, bf16[1,64,1024]{2,1,0:T(8,128)(2,1)S(1)}, u32[]{:S(2)}, u32[]{:S(2)}) %collective-permute-start.22) | collective-permute-done | bytes 131104 | tf_op jit(solution)/shard_map/ppermute | solution.py:64
  (298 shorter events, 160.9 us)
Async XLA Ops:
  36.2 18.0 %collective-permute-start = (bf16[1,4,64,1664]{3,2,1,0:T(8,128)(2,1)S(1)}, bf16[1,4,64,1664]{3,2,1,0:T(8,128)(2,1)}, u32[]{:S(2)}, u32[]{:S(2)}) collective-permute-start(bf16[1,4,64,1664]{3,2,1,0:T(8,128)(2,1)S(1)} %bitcast.482), channel_id=1, source_target_pairs={{0,4},{2,6},{4,0},{6,2},{1,5},{3,7},{5,1},{7,3},{8,12},{10,14},{12... | collective-permute-start | bytes 2555912 | tf_op jit(solution)/shard_map/ppermute | solution.py:64
  56.9 13.2 %collective-permute-start.1 = (bf16[2,4,64,1664]{3,2,1,0:T(8,128)(2,1)}, bf16[2,4,64,1664]{3,2,1,0:T(8,128)(2,1)}, u32[]{:S(2)}, u32[]{:S(2)}) collective-permute-start(bf16[2,4,64,1664]{3,2,1,0:T(8,128)(2,1)} %maximum_bitcast_fusion.1), channel_id=1, source_target_pairs={{0,2},{2,0},{4,6},{6,4},{1,3},{3,1},{5,7},{7,5},{8,10},{10,8},{12,... | collective-permute-start | bytes 5111816 | tf_op jit(solution)/shard_map/ppermute | solution.py:64
  64.4 42.6 %all-to-all-start = ((bf16[4,3,64,1024]{3,2,1,0:T(8,128)(2,1)}), bf16[4,3,64,1024]{3,2,1,0:T(8,128)(2,1)}, u32[]{:S(2)}, u32[]{:S(2)}) async-start(bf16[4,3,64,1024]{3,2,1,0:T(8,128)(2,1)} %copy.340), calls=%async_computation | async-start | bytes 3145728 | tf_op jit(solution)/shard_map/all_to_all | solution.py:196
  69.2 115.8 %all-gather.4.cloned.1.call-start = ((), (), s32[]{:S(2)}) async-start(), calls=%async_computation.4 | async-start | bytes 1474560 | tf_op jit(solution)/shard_map/all_gather | solution.py:181
  114.0 37.2 %collective-permute-start.5 = (bf16[1,4,3,64,1024]{4,3,2,1,0:T(8,128)(2,1)}, bf16[1,4,3,64,1024]{4,3,2,1,0:T(8,128)(2,1)}, u32[]{:S(2)}, u32[]{:S(2)}) collective-permute-start(bf16[1,4,3,64,1024]{4,3,2,1,0:T(8,128)(2,1)} %bitcast.36), channel_id=1, source_target_pairs={{0,4},{2,6},{4,0},{6,2},{1,5},{3,7},{5,1},{7,3},{8,12},{10,14},{12... | collective-permute-start | bytes 4718600 | tf_op jit(solution)/shard_map/ppermute | solution.py:64
  125.4 8.5 %collective-permute-start.4 = (bf16[128,1024]{1,0:T(8,128)(2,1)S(1)}, bf16[128,1024]{1,0:T(8,128)(2,1)S(1)}, u32[]{:S(2)}, u32[]{:S(2)}) collective-permute-start(bf16[128,1024]{1,0:T(8,128)(2,1)S(1)} %get-tuple-element.85), channel_id=1, source_target_pairs={{0,1},{1,0},{2,3},{3,2},{4,5},{5,4},{6,7},{7,6},{8,9},{9,8},{10,11... | collective-permute-start | bytes 786440 | tf_op jit(solution)/shard_map/ppermute | solution.py:64
  155.1 33.7 %collective-permute-start.6 = (bf16[2,4,3,64,1024]{4,3,2,1,0:T(8,128)(2,1)}, bf16[2,4,3,64,1024]{4,3,2,1,0:T(8,128)(2,1)}, u32[]{:S(2)}, u32[]{:S(2)}) collective-permute-start(bf16[2,4,3,64,1024]{4,3,2,1,0:T(8,128)(2,1)} %maximum_bitcast_fusion), channel_id=1, source_target_pairs={{0,2},{2,0},{4,6},{6,4},{1,3},{3,1},{5,7},{7,5},{8,10},{10,8},{12,... | collective-permute-start | bytes 9437192 | tf_op jit(solution)/shard_map/ppermute | solution.py:64
  155.2 59.1 %all-gather.6.cloned.1.call-start = ((), (), s32[]{:S(2)}) async-start(), calls=%async_computation.5 | async-start | bytes 1310720 | tf_op jit(solution)/shard_map/all_gather | solution.py:245
  233.4 51.2 %collective-permute-start.8 = (bf16[4,2,3,64,1024]{4,3,2,1,0:T(8,128)(2,1)}, bf16[4,2,3,64,1024]{4,3,2,1,0:T(8,128)(2,1)}, u32[]{:S(2)}, u32[]{:S(2)}) collective-permute-start(bf16[4,2,3,64,1024]{4,3,2,1,0:T(8,128)(2,1)} %fusion.1), channel_id=1, source_target_pairs={{0,2},{2,0},{4,6},{6,4},{1,3},{3,1},{5,7},{7,5},{8,10},{10,8},{12,... | collective-permute-start | bytes 9437192 | tf_op jit(solution)/shard_map/ppermute | solution.py:64
  235.7 31.0 %all-to-all-start.1 = ((bf16[4,128,1024]{2,1,0:T(8,128)(2,1)}), bf16[4,128,1024]{2,1,0:T(8,128)(2,1)}, u32[]{:S(2)}, u32[]{:S(2)}) async-start(bf16[4,128,1024]{2,1,0:T(8,128)(2,1)} %bitcast.510), calls=%async_computation.1 | async-start | bytes 2097152 | tf_op jit(solution)/shard_map/all_to_all | solution.py:265
  269.8 9.2 %collective-permute-start.7 = (bf16[128,1024]{1,0:T(8,128)(2,1)}, bf16[128,1024]{1,0:T(8,128)(2,1)S(1)}, u32[]{:S(2)}, u32[]{:S(2)}) collective-permute-start(bf16[128,1024]{1,0:T(8,128)(2,1)} %reduce-precision_convert_fusion.2), channel_id=1, source_target_pairs={{0,1},{1,0},{2,3},{3,2},{4,5},{5,4},{6,7},{7,6},{8,9},{9,8},{10,11... | collective-permute-start | bytes 786440 | tf_op jit(solution)/shard_map/ppermute | solution.py:64
  274.8 94.0 %all-to-all-start.2 = ((bf16[4,128,1024]{2,1,0:T(8,128)(2,1)}), bf16[4,128,1024]{2,1,0:T(8,128)(2,1)}, u32[]{:S(2)}, u32[]{:S(2)}) async-start(bf16[4,128,1024]{2,1,0:T(8,128)(2,1)} %bitcast.509), calls=%async_computation.2 | async-start | bytes 2097152 | tf_op jit(solution)/shard_map/all_to_all | solution.py:269
  304.9 10.1 %collective-permute-start.23 = (bf16[4,2,64,512]{3,2,1,0:T(8,128)(2,1)}, bf16[4,2,64,512]{3,2,1,0:T(8,128)(2,1)}, u32[]{:S(2)}, u32[]{:S(2)}) collective-permute-start(bf16[4,2,64,512]{3,2,1,0:T(8,128)(2,1)} %fusion.31), channel_id=1, source_target_pairs={{0,2},{2,0},{4,6},{6,4},{1,3},{3,1},{5,7},{7,5},{8,10},{10,8},{12,... | collective-permute-start | bytes 1572872 | tf_op jit(solution)/shard_map/ppermute | solution.py:64
  309.7 48.0 %collective-permute-start.9 = (bf16[2,128,512]{2,1,0:T(8,128)(2,1)}, bf16[2,128,512]{2,1,0:T(8,128)(2,1)S(1)}, u32[]{:S(2)}, u32[]{:S(2)}) collective-permute-start(bf16[2,128,512]{2,1,0:T(8,128)(2,1)} %bitcast.519), channel_id=1, source_target_pairs={{0,2},{2,0},{4,6},{6,4},{1,3},{3,1},{5,7},{7,5},{8,10},{10,8},{12,... | collective-permute-start | bytes 786440 | tf_op jit(solution)/shard_map/ppermute | solution.py:64
  313.5 53.2 %collective-permute-start.11 = (bf16[4,1,3,64,1024]{4,3,2,0,1:T(8,128)(2,1)S(1)}, bf16[4,1,3,64,1024]{4,3,2,0,1:T(8,128)(2,1)S(1)}, u32[]{:S(2)}, u32[]{:S(2)}) collective-permute-start(bf16[4,1,3,64,1024]{4,3,2,0,1:T(8,128)(2,1)S(1)} %fusion.13), channel_id=1, source_target_pairs={{0,4},{2,6},{4,0},{6,2},{1,5},{3,7},{5,1},{7,3},{8,12},{10,14},{12... | collective-permute-start | bytes 4718600 | tf_op jit(solution)/shard_map/ppermute | solution.py:64
  317.1 38.4 %collective-permute-start.24 = (bf16[4,1,64,512]{3,2,0,1:T(8,128)(2,1)S(1)}, bf16[4,1,64,512]{3,2,0,1:T(8,128)(2,1)S(1)}, u32[]{:S(2)}, u32[]{:S(2)}) collective-permute-start(bf16[4,1,64,512]{3,2,0,1:T(8,128)(2,1)S(1)} %fusion.52), channel_id=1, source_target_pairs={{0,4},{2,6},{4,0},{6,2},{1,5},{3,7},{5,1},{7,3},{8,12},{10,14},{12... | collective-permute-start | bytes 786440 | tf_op jit(solution)/shard_map/ppermute | solution.py:64
  378.9 10.4 %collective-permute-start.13 = (bf16[128,1024]{1,0:T(8,128)(2,1)}, bf16[128,1024]{1,0:T(8,128)(2,1)S(1)}, u32[]{:S(2)}, u32[]{:S(2)}) collective-permute-start(bf16[128,1024]{1,0:T(8,128)(2,1)} %get-tuple-element.87), channel_id=1, source_target_pairs={{0,1},{1,0},{2,3},{3,2},{4,5},{5,4},{6,7},{7,6},{8,9},{9,8},{10,11... | collective-permute-start | bytes 786440 | tf_op jit(solution)/shard_map/ppermute | solution.py:64
  381.0 53.8 %all-to-all-start.3 = ((bf16[4,3,64,1024]{3,2,1,0:T(8,128)(2,1)}), bf16[4,3,64,1024]{3,2,1,0:T(8,128)(2,1)}, u32[]{:S(2)}, u32[]{:S(2)}) async-start(bf16[4,3,64,1024]{3,2,1,0:T(8,128)(2,1)} %fusion.14), calls=%async_computation.3 | async-start | bytes 3145728 | tf_op jit(solution)/shard_map/all_to_all | solution.py:312
  392.0 10.2 %collective-permute-start.19 = (bf16[4,2,64,1024]{3,2,1,0:T(8,128)(2,1)S(1)}, bf16[4,2,64,1024]{3,2,1,0:T(8,128)(2,1)S(1)}, u32[]{:S(2)}, u32[]{:S(2)}) collective-permute-start(bf16[4,2,64,1024]{3,2,1,0:T(8,128)(2,1)S(1)} %fusion.16), channel_id=1, source_target_pairs={{0,2},{2,0},{4,6},{6,4},{1,3},{3,1},{5,7},{7,5},{8,10},{10,8},{12,... | collective-permute-start | bytes 3145736 | tf_op jit(solution)/shard_map/ppermute | solution.py:64
  400.1 9.3 %collective-permute-start.16 = (bf16[2,1,128]{2,0,1:T(2,128)(2,1)S(1)}, bf16[2,1,128]{2,0,1:T(2,128)(2,1)S(1)}, u32[]{:S(2)}, u32[]{:S(2)}) collective-permute-start(bf16[2,1,128]{2,0,1:T(2,128)(2,1)S(1)} %bitcast.533), channel_id=1, source_target_pairs={{0,8},{8,0},{16,24},{24,16},{1,9},{9,1},{17,25},{25,17},{2,10},{10... | collective-permute-start | bytes 1544 | tf_op jit(solution)/shard_map/ppermute | solution.py:64
  402.9 11.1 %collective-permute-start.20 = (bf16[4,1,64,1024]{3,2,0,1:T(8,128)(2,1)S(1)}, bf16[4,1,64,1024]{3,2,0,1:T(8,128)(2,1)S(1)}, u32[]{:S(2)}, u32[]{:S(2)}) collective-permute-start(bf16[4,1,64,1024]{3,2,0,1:T(8,128)(2,1)S(1)} %fusion.30), channel_id=1, source_target_pairs={{0,4},{2,6},{4,0},{6,2},{1,5},{3,7},{5,1},{7,3},{8,12},{10,14},{12... | collective-permute-start | bytes 1572872 | tf_op jit(solution)/shard_map/ppermute | solution.py:64
  409.4 11.6 %collective-permute-start.17 = (bf16[1,1,128]{2,1,0:T(2,128)(2,1)S(1)}, bf16[1,1,128]{2,1,0:T(2,128)(2,1)S(1)}, u32[]{:S(2)}, u32[]{:S(2)}) collective-permute-start(bf16[1,1,128]{2,1,0:T(2,128)(2,1)S(1)} %fusion.76), channel_id=1, source_target_pairs={{0,16},{8,24},{16,0},{24,8},{1,17},{9,25},{17,1},{25,9},{2,18},{10... | collective-permute-start | bytes 776 | tf_op jit(solution)/shard_map/ppermute | solution.py:64
  414.3 11.5 %collective-permute-start.21 = (bf16[2,64,1024]{2,1,0:T(8,128)(2,1)S(1)}, bf16[2,64,1024]{2,1,0:T(8,128)(2,1)S(1)}, u32[]{:S(2)}, u32[]{:S(2)}) collective-permute-start(bf16[2,64,1024]{2,1,0:T(8,128)(2,1)S(1)} %fusion.51), channel_id=1, source_target_pairs={{0,8},{8,0},{16,24},{24,16},{1,9},{9,1},{17,25},{25,17},{2,10},{10... | collective-permute-start | bytes 786440 | tf_op jit(solution)/shard_map/ppermute | solution.py:64
  426.0 7.5 %collective-permute-start.22 = (bf16[1,64,1024]{2,1,0:T(8,128)(2,1)S(1)}, bf16[1,64,1024]{2,1,0:T(8,128)(2,1)S(1)}, u32[]{:S(2)}, u32[]{:S(2)}) collective-permute-start(bf16[1,64,1024]{2,1,0:T(8,128)(2,1)S(1)} %fusion.61), channel_id=1, source_target_pairs={{0,16},{8,24},{16,0},{24,8},{1,17},{9,25},{17,1},{25,9},{2,18},{10... | collective-permute-start | bytes 393224 | tf_op jit(solution)/shard_map/ppermute | solution.py:64
  (52 other events, 596.0 us)
Sparse Core Ops, SparseCore 0:
  155.3 29.6 all-gather.3
  187.2 27.0 all-gather.5

commit v3 on v2

--- a/solution.py
+++ b/solution.py
@@ -159,7 +159,9 @@
     packed = jnp.concatenate(
         [query_weight, key_weight, value_matrix, output_weight, gains], axis=1
     )
-    packed_all = lax.all_gather(packed, "shard", axis=0, tiled=False)
+    packed_all = packed[None]
+    for bit in reversed(axis_bits("shard")):
+        packed_all = ordered_step(packed_all, "shard", bit)
 
     grad_out = cotangent[0]
     expert_ids = jnp.arange(experts, dtype=jnp.int32)
@@ -177,24 +179,25 @@
         ],
         axis=1,
     )
-    packed_all, early = tie(packed_all, early)
-    early_all = lax.all_gather(early, "shard", axis=0, tiled=True)
-
+
+    stacked_weights = jnp.stack([gate_weight, up_weight, down_weight], axis=0)
+    stacked_weights = stacked_weights.reshape(3, rows_own, shard_count, own_cols)
+    stacked_weights = jnp.transpose(stacked_weights, (2, 0, 1, 3))
+    owner = lax.all_to_all(stacked_weights, "shard", split_axis=0, concat_axis=0, tiled=True)
     bits = axis_bits("context")
     full = packed_all[None]
-    for bit in reversed(bits):
+    for bit in reversed(bits[1:]):
         full = ordered_step(full, "context", bit)
+    full, owner, early = tie(full, owner, early)
+    full = ordered_step(full, "context", 1)
     full = jnp.swapaxes(full, 0, 1).reshape(model_width, packed.shape[1])
     qkv_full = full[:, :qkv_cols]
     output_full = full[:, qkv_cols : qkv_cols + q_cols]
     gain_rows = full[:, qkv_cols + q_cols :].astype(f32).T
     gain_attn, gain_ffn = gain_rows[0], gain_rows[1]
-
-    stacked_weights = jnp.stack([gate_weight, up_weight, down_weight], axis=0)
-    stacked_weights = stacked_weights.reshape(3, rows_own, shard_count, own_cols)
-    stacked_weights = jnp.transpose(stacked_weights, (2, 0, 1, 3))
-    owner = lax.all_to_all(stacked_weights, "shard", split_axis=0, concat_axis=0, tiled=True)
-    qkv_full, owner = tie(qkv_full, owner)
+    early_all = early[None]
+    for bit in reversed(axis_bits("shard")):
+        early_all = ordered_step(early_all, "shard", bit)
     expert_blocks = owner[None]
     for bit in reversed(bits[1:]):
         expert_blocks = ordered_step(expert_blocks, "context", bit)
@@ -236,7 +239,8 @@
     scale_two = inverse_rms(hidden)
     normed_two = (hidden * scale_two * gain_ffn).astype(b16)
 
-    normed_two, expert_blocks = tie(normed_two, expert_blocks)
+    normed_two, expert_blocks, early_all = tie(normed_two, expert_blocks, early_all)
+    early_all = early_all.reshape(shard_count * length, -1)
     expert_blocks = ordered_step(expert_blocks, "context", 1)
     expert_weights = jnp.transpose(expert_blocks, (2, 1, 0, 3, 4)).reshape(
         3, model_width, own_cols
@@ -266,10 +270,6 @@
         normed_two_terms.reshape(shard_count, length, model_width), "shard", 0, 0, tiled=True
     )
     moe_terms = contract_cols(activated, own_down).astype(b16)
-    moe_parts = lax.all_to_all(
-        moe_terms.reshape(shard_count, length, model_width), "shard", 0, 0, tiled=True
-    )
-    grad_normed_two = pair_sum(jnp.sum(normed_two_parts.astype(f32), axis=0), "tensor")
 
     expert_terms = jnp.stack(
         [
@@ -282,12 +282,16 @@
     expert_terms = jnp.transpose(
         expert_terms.reshape(3, shard_count, context_count, rows_own, own_cols), (1, 2, 0, 3, 4)
     )
-    expert_terms = halving_step(expert_terms, "context", 1, 1)
+    expert_terms = halving_step(expert_terms, "context", 1, 1).astype(b16)
+    normed_two_parts, expert_terms, moe_terms = tie(normed_two_parts, expert_terms, moe_terms)
+    moe_parts = lax.all_to_all(
+        moe_terms.reshape(shard_count, length, model_width), "shard", 0, 0, tiled=True
+    )
+    grad_normed_two = pair_sum(jnp.sum(normed_two_parts.astype(f32), axis=0), "tensor")
 
     term_ffn_gain = jnp.sum(grad_normed_two * hidden * scale_two, axis=0)
     grad_hidden = grad_out + norm_backward(grad_normed_two, hidden, scale_two, gain_ffn)
     grad_attn = (RESIDUAL_SCALE * grad_hidden).astype(b16)
-    grad_attn, expert_terms = tie(grad_attn, expert_terms)
     for bit in bits[1:]:
         expert_terms = halving_step(expert_terms, "context", 1, bit)
     context_sums = expert_terms[:, 0].astype(b16)
@@ -305,8 +309,9 @@
     kv_terms = jnp.concatenate(
         [key_term.reshape(-1, kv_cols), value_term.reshape(-1, kv_cols)], axis=1
     ).reshape(context_count, length, 2 * kv_cols)
+    kv_terms, context_sums = tie(kv_terms, context_sums)
     kv_sum = relative_sum(kv_terms, "context")
-    kv_sum, moe_parts, context_sums = tie(kv_sum, moe_parts, context_sums)
+    kv_sum, moe_parts = tie(kv_sum, moe_parts)
     moe = pair_sum(jnp.sum(moe_parts.astype(f32), axis=0), "tensor")
     output = hidden + RESIDUAL_SCALE * moe
     expert_sums = lax.all_to_all(context_sums, "shard", 0, 0, tiled=True)

time: 459 us -> 362 us (0.79)
  waiting for transfers between devices: 213 us -> 142 us
  blocking collectives: 22.1 us -> 0 us
  other arithmetic: 65.5 us -> 54.5 us
  local copies, waits for them, and re-layouts: 47.1 us -> 55.4 us
    all_gather x1 -> x0, waiting for transfers between devices: 29.1 us -> none  [body(): early_all = lax.all_gather(early, 'shard', axis=0, tiled=True)]
    all_gather x1 -> x0, blocking collectives: 22.1 us -> none  [body(): packed_all = lax.all_gather(packed, 'shard', axis=0, tiled=False)]
    all_to_all x1, waiting for transfers between devices: 32.2 us -> 15.7 us  [body(): lax.all_to_all(stacked_weights, 'shard', split_axis=0, concat_axis=0, til...]
    ppermute x27 -> x31, waiting for transfers between devices: 108 us -> 96.7 us  [exchange(): return lax.ppermute(array, axis, [(i, i ^ bit) for i in range(size)])]
    all_to_all x1, waiting for transfers between devices: 26.7 us -> 16.9 us  [body(): lax.all_to_all(normed_two_terms.reshape(shard_count, length, model_width)...]
    add x4 -> x3, other arithmetic: 9.23 us -> 0.39 us  [halving_step(): kept.astype(jnp.float32) + exchange(sent, axis, bit).astype(jnp.float32)]
    concatenate x0 -> x4, local copies, waits for them, and re-layouts: none -> 8.1 us  [body(): jnp.concatenate([key_term.reshape(-1, kv_cols), value_term.reshape(-1, kv...]
    ppermute x27 -> x31, starting transfers between devices: 31 us -> 34.5 us  [exchange(): return lax.ppermute(array, axis, [(i, i ^ bit) for i in range(size)])]
  transfers between devices with their start and end apart: 33 -> 36, of which waited for: 18 -> 23; matrix products, arithmetic and copies ran while one was open for 21% -> 32% of each run, Pallas kernels for 0% -> 0%
where the time goes in v3:
time: 362 us; the launch traced here: 357 us
  waiting for transfers between devices  142 us (39%)
  local copies, waits for them, and re-layouts  55.4 us (15%)
  other arithmetic  54.5 us (15%)
  starting transfers between devices  53.4 us (15%)
  matrix products  36.2 us (10%)
  between operations  15.6 us (4%)
    ppermute x31, waiting for transfers between devices, exchange(): return lax.ppermute(array, axis, [(i, i ^ bit) for i in range(size)])  96.7 us
    ppermute x31, starting transfers between devices, exchange(): return lax.ppermute(array, axis, [(i, i ^ bit) for i in range(size)])  34.5 us
    all_to_all x1, waiting for transfers between devices, body(): lax.all_to_all(normed_two_terms.reshape(shard_count, length, model_width)...  16.9 us
    all_to_all x1, waiting for transfers between devices, body(): lax.all_to_all(stacked_weights, 'shard', split_axis=0, concat_axis=0, til...  15.7 us
    all_gather x1, waiting for transfers between devices, body(): x_all = lax.all_gather(normed_two, 'shard', axis=0, tiled=True)  12.8 us
    unnamed x133, local copies, waits for them, and re-layouts  12.2 us
    dot_general x5, matrix products, contract_cols(): lax.dot_general(left, right, (((1,), (1,)), ((), ())), preferred_element_...  9.87 us
    another operation x12, other arithmetic, ordered_step(): return jnp.stack([low, high], axis=1).reshape((-1,) + blocks.shape[1:])  8.59 us
  transfers between devices with their start and end apart: 36, of which 23 were waited for; matrix products, arithmetic and copies ran while one was open for 32% of the time, Pallas kernels for 0%

profile of v3, /device:TPU:0, one launch (start us, length us, event | category | flops | bytes accessed | tf_op | source)
XLA Modules:
  0.0 357.2 jit_solution(1611860591557489326)
XLA Ops:
  11.4 4.1 %collective-permute-start = (bf16[1,64,1664]{2,1,0:T(8,128)(2,1)S(1)}, bf16[1,64,1664]{2,1,0:T(8,128)(2,1)S(1)}, u32[]{:S(2)}, u32[]{:S(2)}) collective-permute-start(bf16[1,64,1664]{2,1,0:T(8,128)(2,1)S(1)} %bitcast.540), channel_id=1, source_target_pairs={{0,16},{8,24},{16,0},{24,8},{1,17},{9,25},{17,1},{25,9},{2,18},{10... | collective-permute-start | bytes 638984 | tf_op jit(solution)/shard_map/ppermute | solution.py:64
  15.5 9.8 %collective-permute-done = bf16[1,64,1664]{2,1,0:T(8,128)(2,1)S(1)} collective-permute-done((bf16[1,64,1664]{2,1,0:T(8,128)(2,1)S(1)}, bf16[1,64,1664]{2,1,0:T(8,128)(2,1)S(1)}, u32[]{:S(2)}, u32[]{:S(2)}) %collective-permute-start) | collective-permute-done | bytes 213024 | tf_op jit(solution)/shard_map/ppermute | solution.py:64
  30.4 4.8 %all-to-all-start = ((bf16[4,3,64,1024]{3,2,1,0:T(8,128)(2,1)}), bf16[4,3,64,1024]{3,2,1,0:T(8,128)(2,1)}, u32[]{:S(2)}, u32[]{:S(2)}) async-start(bf16[4,3,64,1024]{3,2,1,0:T(8,128)(2,1)} %copy.347), calls=%async_computation | async-start | bytes 3145728 | tf_op jit(solution)/shard_map/all_to_all | solution.py:186
  40.9 15.9 %collective-permute-done.2 = bf16[1,4,64,1664]{3,2,1,0:T(8,128)(2,1)S(1)} collective-permute-done((bf16[1,4,64,1664]{3,2,1,0:T(8,128)(2,1)S(1)}, bf16[1,4,64,1664]{3,2,1,0:T(8,128)(2,1)S(1)}, u32[]{:S(2)}, u32[]{:S(2)}) %collective-permute-start.2) | collective-permute-done | bytes 852000 | tf_op jit(solution)/shard_map/ppermute | solution.py:64
  57.2 15.7 %all-to-all-done = bf16[4,3,64,1024]{3,2,1,0:T(8,128)(2,1)} async-done(((bf16[4,3,64,1024]{3,2,1,0:T(8,128)(2,1)}), bf16[4,3,64,1024]{3,2,1,0:T(8,128)(2,1)}, u32[]{:S(2)}, u32[]{:S(2)}) %all-to-all-start) | async-done | bytes 1572896 | tf_op jit(solution)/shard_map/all_to_all | solution.py:186
  75.4 12.6 %collective-permute-done.8 = bf16[1,128,1152]{2,1,0:T(8,128)(2,1)S(1)} collective-permute-done((bf16[1,128,1152]{2,1,0:T(8,128)(2,1)}, bf16[1,128,1152]{2,1,0:T(8,128)(2,1)S(1)}, u32[]{:S(2)}, u32[]{:S(2)}) %collective-permute-start.8) | collective-permute-done | bytes 294944 | tf_op jit(solution)/shard_map/ppermute | solution.py:64
  101.3 4.4 %collective-permute-done.9 = bf16[2,128,1152]{2,1,0:T(8,128)(2,1)} collective-permute-done((bf16[2,128,1152]{2,1,0:T(8,128)(2,1)}, bf16[2,128,1152]{2,1,0:T(8,128)(2,1)}, u32[]{:S(2)}, u32[]{:S(2)}) %collective-permute-start.9) | collective-permute-done | bytes 589856 | tf_op jit(solution)/shard_map/ppermute | solution.py:64
  107.0 6.7 %collective-permute-done.4 = bf16[1,128,512]{2,1,0:T(8,128)(2,1)S(1)} collective-permute-done((bf16[1,128,512]{2,1,0:T(8,128)(2,1)S(1)}, bf16[1,128,512]{2,1,0:T(8,128)(2,1)S(1)}, u32[]{:S(2)}, u32[]{:S(2)}) %collective-permute-start.4) | collective-permute-done | bytes 131104 | tf_op jit(solution)/shard_map/ppermute | solution.py:64
  119.9 3.3 fusion.95
  129.9 4.5 %collective-permute-done.6 = bf16[128,1024]{1,0:T(8,128)(2,1)S(1)} collective-permute-done((bf16[128,1024]{1,0:T(8,128)(2,1)S(1)}, bf16[128,1024]{1,0:T(8,128)(2,1)S(1)}, u32[]{:S(2)}, u32[]{:S(2)}) %collective-permute-start.6) | collective-permute-done | bytes 262176 | tf_op jit(solution)/shard_map/ppermute | solution.py:64
  138.6 3.4 collective-permute-done.10
  152.0 12.8 %all-gather.2.cloned.1.call-done = bf16[512,1024]{1,0:T(8,128)(2,1)} async-done(((bf16[128,1024]{1,0:T(8,128)(2,1)}), bf16[512,1024]{1,0:T(8,128)(2,1)}) %all-gather.2.cloned.1.call-update) | async-done | bytes 1048592 | tf_op jit(solution)/shard_map/all_gather | solution.py:249
  164.8 3.3 fusion.97
  182.8 4.7 %all-to-all-start.1 = ((bf16[4,128,1024]{2,1,0:T(8,128)(2,1)}), bf16[4,128,1024]{2,1,0:T(8,128)(2,1)}, u32[]{:S(2)}, u32[]{:S(2)}) async-start(bf16[4,128,1024]{2,1,0:T(8,128)(2,1)} %bitcast.62), calls=%async_computation.1 | async-start | bytes 2097152 | tf_op jit(solution)/shard_map/all_to_all | solution.py:269
  187.6 4.0 %convolution_convert_fusion.2 = bf16[512,1024]{1,0:T(8,128)(2,1)} fusion(bf16[512,1024]{1,0:T(8,128)(2,1)S(1)} %copy-done.59, bf16[1024,1024]{1,0:T(8,128)(2,1)} %bitcast.509), kind=kOutput, calls=%fused_computation.54 | convolution fusion | flops 1074266112 | bytes 4194304 | tf_op jit(solution)/shard_map/dot_general | solution.py:57
  191.6 5.8 %fusion.1 = bf16[4,2,3,64,1024]{4,3,2,1,0:T(8,128)(2,1)} fusion(bf16[4,2,3,64,1024]{4,3,2,1,0:T(8,128)(2,1)} %collective-permute-done.11, pred[]{:T(512)S(6)} %eq.39, bf16[4,2,2,3,64,1024]{5,4,3,2,1,0:T(8,128)(2,1)S(1)} %bitcast.487), kind=kLoop, calls=%fused_computation.4 | loop fusion | flops 7864320 | bytes 12582913 | tf_op jit(solution)/shard_map/convert_element_type | solution.py:285
  197.4 16.9 %all-to-all-done.1 = bf16[4,128,1024]{2,1,0:T(8,128)(2,1)} async-done(((bf16[4,128,1024]{2,1,0:T(8,128)(2,1)}), bf16[4,128,1024]{2,1,0:T(8,128)(2,1)}, u32[]{:S(2)}, u32[]{:S(2)}) %all-to-all-start.1) | async-done | bytes 1048608 | tf_op jit(solution)/shard_map/all_to_all | solution.py:269
  216.6 4.3 %all-to-all-start.2 = ((bf16[4,128,1024]{2,1,0:T(8,128)(2,1)}), bf16[4,128,1024]{2,1,0:T(8,128)(2,1)}, u32[]{:S(2)}, u32[]{:S(2)}) async-start(bf16[4,128,1024]{2,1,0:T(8,128)(2,1)} %bitcast.532), calls=%async_computation.2 | async-start | bytes 2097152 | tf_op jit(solution)/shard_map/all_to_all | solution.py:287
  226.3 3.6 %collective-permute-done.12 = bf16[128,1024]{1,0:T(8,128)(2,1)S(1)} collective-permute-done((bf16[128,1024]{1,0:T(8,128)(2,1)S(1)}, bf16[128,1024]{1,0:T(8,128)(2,1)S(1)}, u32[]{:S(2)}, u32[]{:S(2)}) %collective-permute-start.12) | collective-permute-done | bytes 262176 | tf_op jit(solution)/shard_map/ppermute | solution.py:64
  258.2 8.2 %collective-permute-done.28 = bf16[4,1,64,512]{3,2,0,1:T(8,128)(2,1)S(1)} collective-permute-done((bf16[4,1,64,512]{3,2,0,1:T(8,128)(2,1)S(1)}, bf16[4,1,64,512]{3,2,0,1:T(8,128)(2,1)S(1)}, u32[]{:S(2)}, u32[]{:S(2)}) %collective-permute-start.28) | collective-permute-done | bytes 262176 | tf_op jit(solution)/shard_map/ppermute | solution.py:64
  268.3 3.6 %fusion.17 = bf16[4,3,64,1024]{3,2,1,0:T(8,128)(2,1)} fusion(bf16[4,1,3,64,1024]{4,3,2,0,1:T(8,128)(2,1)} %collective-permute-done.13, pred[]{:T(512)S(6)} %eq.40, bf16[4,1,2,3,64,1024]{5,4,3,2,0,1:T(8,128)(2,1)S(1)} %bitcast.489), kind=kLoop, calls=%fused_computation.48 | loop fusion | flops 3932160 | bytes 6291457 | tf_op jit(solution)/shard_map/convert_element_type | solution.py:297
  281.1 4.6 %all-to-all-start.3 = ((bf16[4,3,64,1024]{3,2,1,0:T(8,128)(2,1)}), bf16[4,3,64,1024]{3,2,1,0:T(8,128)(2,1)}, u32[]{:S(2)}, u32[]{:S(2)}) async-start(bf16[4,3,64,1024]{3,2,1,0:T(8,128)(2,1)} %fusion.17), calls=%async_computation.3 | async-start | bytes 3145728 | tf_op jit(solution)/shard_map/all_to_all | solution.py:317
  300.0 5.6 %collective-permute-done.17 = bf16[128,1024]{1,0:T(8,128)(2,1)S(1)} collective-permute-done((bf16[128,1024]{1,0:T(8,128)(2,1)S(1)}, bf16[128,1024]{1,0:T(8,128)(2,1)S(1)}, u32[]{:S(2)}, u32[]{:S(2)}) %collective-permute-start.17) | collective-permute-done | bytes 262176 | tf_op jit(solution)/shard_map/ppermute | solution.py:64
  327.0 6.4 %collective-permute-done.24 = bf16[4,1,64,1024]{3,2,0,1:T(8,128)(2,1)S(1)} collective-permute-done((bf16[4,1,64,1024]{3,2,0,1:T(8,128)(2,1)S(1)}, bf16[4,1,64,1024]{3,2,0,1:T(8,128)(2,1)S(1)}, u32[]{:S(2)}, u32[]{:S(2)}) %collective-permute-start.24) | collective-permute-done | bytes 524320 | tf_op jit(solution)/shard_map/ppermute | solution.py:64
  (351 shorter events, 172.5 us)
Async XLA Ops:
  11.4 13.9 %collective-permute-start = (bf16[1,64,1664]{2,1,0:T(8,128)(2,1)S(1)}, bf16[1,64,1664]{2,1,0:T(8,128)(2,1)S(1)}, u32[]{:S(2)}, u32[]{:S(2)}) collective-permute-start(bf16[1,64,1664]{2,1,0:T(8,128)(2,1)S(1)} %bitcast.540), channel_id=1, source_target_pairs={{0,16},{8,24},{16,0},{24,8},{1,17},{9,25},{17,1},{25,9},{2,18},{10... | collective-permute-start | bytes 638984 | tf_op jit(solution)/shard_map/ppermute | solution.py:64
  26.1 11.2 %collective-permute-start.1 = (bf16[2,64,1664]{2,1,0:T(8,128)(2,1)}, bf16[2,64,1664]{2,1,0:T(8,128)(2,1)S(1)}, u32[]{:S(2)}, u32[]{:S(2)}) collective-permute-start(bf16[2,64,1664]{2,1,0:T(8,128)(2,1)} %maximum_bitcast_fusion.4), channel_id=1, source_target_pairs={{0,8},{8,0},{16,24},{24,16},{1,9},{9,1},{17,25},{25,17},{2,10},{10... | collective-permute-start | bytes 1277960 | tf_op jit(solution)/shard_map/ppermute | solution.py:64
  30.4 42.4 %all-to-all-start = ((bf16[4,3,64,1024]{3,2,1,0:T(8,128)(2,1)}), bf16[4,3,64,1024]{3,2,1,0:T(8,128)(2,1)}, u32[]{:S(2)}, u32[]{:S(2)}) async-start(bf16[4,3,64,1024]{3,2,1,0:T(8,128)(2,1)} %copy.347), calls=%async_computation | async-start | bytes 3145728 | tf_op jit(solution)/shard_map/all_to_all | solution.py:186
  35.2 129.6 %all-gather.2.cloned.1.call-start = ((), (), s32[]{:S(2)}) async-start(), calls=%async_computation.4 | async-start | bytes 1310720 | tf_op jit(solution)/shard_map/all_gather | solution.py:249
  37.6 19.3 %collective-permute-start.2 = (bf16[1,4,64,1664]{3,2,1,0:T(8,128)(2,1)S(1)}, bf16[1,4,64,1664]{3,2,1,0:T(8,128)(2,1)S(1)}, u32[]{:S(2)}, u32[]{:S(2)}) collective-permute-start(bf16[1,4,64,1664]{3,2,1,0:T(8,128)(2,1)S(1)} %bitcast.502), channel_id=1, source_target_pairs={{0,4},{2,6},{4,0},{6,2},{1,5},{3,7},{5,1},{7,3},{8,12},{10,14},{12... | collective-permute-start | bytes 2555912 | tf_op jit(solution)/shard_map/ppermute | solution.py:64
  72.9 17.2 %collective-permute-start.3 = (bf16[2,4,64,1664]{3,2,1,0:T(8,128)(2,1)S(1)}, bf16[2,4,64,1664]{3,2,1,0:T(8,128)(2,1)S(1)}, u32[]{:S(2)}, u32[]{:S(2)}) collective-permute-start(bf16[2,4,64,1664]{3,2,1,0:T(8,128)(2,1)S(1)} %maximum_bitcast_fusion.1), channel_id=1, source_target_pairs={{0,2},{2,0},{4,6},{6,4},{1,3},{3,1},{5,7},{7,5},{8,10},{10,8},{12,... | collective-permute-start | bytes 5111816 | tf_op jit(solution)/shard_map/ppermute | solution.py:64
  73.0 15.0 %collective-permute-start.8 = (bf16[1,128,1152]{2,1,0:T(8,128)(2,1)}, bf16[1,128,1152]{2,1,0:T(8,128)(2,1)S(1)}, u32[]{:S(2)}, u32[]{:S(2)}) collective-permute-start(bf16[1,128,1152]{2,1,0:T(8,128)(2,1)} %bitcast.525), channel_id=1, source_target_pairs={{0,16},{8,24},{16,0},{24,8},{1,17},{9,25},{17,1},{25,9},{2,18},{10... | collective-permute-start | bytes 884744 | tf_op jit(solution)/shard_map/ppermute | solution.py:64
  73.9 53.6 %collective-permute-start.7 = (bf16[1,4,3,64,1024]{4,3,2,1,0:T(8,128)(2,1)}, bf16[1,4,3,64,1024]{4,3,2,1,0:T(8,128)(2,1)}, u32[]{:S(2)}, u32[]{:S(2)}) collective-permute-start(bf16[1,4,3,64,1024]{4,3,2,1,0:T(8,128)(2,1)} %bitcast.41), channel_id=1, source_target_pairs={{0,4},{2,6},{4,0},{6,2},{1,5},{3,7},{5,1},{7,3},{8,12},{10,14},{12... | collective-permute-start | bytes 4718600 | tf_op jit(solution)/shard_map/ppermute | solution.py:64
  90.0 15.6 %collective-permute-start.9 = (bf16[2,128,1152]{2,1,0:T(8,128)(2,1)}, bf16[2,128,1152]{2,1,0:T(8,128)(2,1)}, u32[]{:S(2)}, u32[]{:S(2)}) collective-permute-start(bf16[2,128,1152]{2,1,0:T(8,128)(2,1)} %maximum_bitcast_fusion.3), channel_id=1, source_target_pairs={{0,8},{8,0},{16,24},{24,16},{1,9},{9,1},{17,25},{25,17},{2,10},{10... | collective-permute-start | bytes 1769480 | tf_op jit(solution)/shard_map/ppermute | solution.py:64
  99.7 14.0 %collective-permute-start.4 = (bf16[1,128,512]{2,1,0:T(8,128)(2,1)S(1)}, bf16[1,128,512]{2,1,0:T(8,128)(2,1)S(1)}, u32[]{:S(2)}, u32[]{:S(2)}) collective-permute-start(bf16[1,128,512]{2,1,0:T(8,128)(2,1)S(1)} %maximum_bitcast_fusion.5), channel_id=1, source_target_pairs={{0,4},{2,6},{4,0},{6,2},{1,5},{3,7},{5,1},{7,3},{8,12},{10,14},{12... | collective-permute-start | bytes 393224 | tf_op jit(solution)/shard_map/ppermute | solution.py:64
  126.0 8.4 %collective-permute-start.6 = (bf16[128,1024]{1,0:T(8,128)(2,1)S(1)}, bf16[128,1024]{1,0:T(8,128)(2,1)S(1)}, u32[]{:S(2)}, u32[]{:S(2)}) collective-permute-start(bf16[128,1024]{1,0:T(8,128)(2,1)S(1)} %get-tuple-element.97), channel_id=1, source_target_pairs={{0,1},{1,0},{2,3},{3,2},{4,5},{5,4},{6,7},{7,6},{8,9},{9,8},{10,11... | collective-permute-start | bytes 786440 | tf_op jit(solution)/shard_map/ppermute | solution.py:64
  179.2 12.4 %collective-permute-start.11 = (bf16[4,2,3,64,1024]{4,3,2,1,0:T(8,128)(2,1)}, bf16[4,2,3,64,1024]{4,3,2,1,0:T(8,128)(2,1)}, u32[]{:S(2)}, u32[]{:S(2)}) collective-permute-start(bf16[4,2,3,64,1024]{4,3,2,1,0:T(8,128)(2,1)} %fusion.2), channel_id=1, source_target_pairs={{0,2},{2,0},{4,6},{6,4},{1,3},{3,1},{5,7},{7,5},{8,10},{10,8},{12,... | collective-permute-start | bytes 9437192 | tf_op jit(solution)/shard_map/ppermute | solution.py:64
  182.8 31.5 %all-to-all-start.1 = ((bf16[4,128,1024]{2,1,0:T(8,128)(2,1)}), bf16[4,128,1024]{2,1,0:T(8,128)(2,1)}, u32[]{:S(2)}, u32[]{:S(2)}) async-start(bf16[4,128,1024]{2,1,0:T(8,128)(2,1)} %bitcast.62), calls=%async_computation.1 | async-start | bytes 2097152 | tf_op jit(solution)/shard_map/all_to_all | solution.py:269
  216.6 64.6 %all-to-all-start.2 = ((bf16[4,128,1024]{2,1,0:T(8,128)(2,1)}), bf16[4,128,1024]{2,1,0:T(8,128)(2,1)}, u32[]{:S(2)}, u32[]{:S(2)}) async-start(bf16[4,128,1024]{2,1,0:T(8,128)(2,1)} %bitcast.532), calls=%async_computation.2 | async-start | bytes 2097152 | tf_op jit(solution)/shard_map/all_to_all | solution.py:287
  221.9 8.0 %collective-permute-start.12 = (bf16[128,1024]{1,0:T(8,128)(2,1)S(1)}, bf16[128,1024]{1,0:T(8,128)(2,1)S(1)}, u32[]{:S(2)}, u32[]{:S(2)}) collective-permute-start(bf16[128,1024]{1,0:T(8,128)(2,1)S(1)} %reduce-precision_convert_fusion.2), channel_id=1, source_target_pairs={{0,1},{1,0},{2,3},{3,2},{4,5},{5,4},{6,7},{7,6},{8,9},{9,8},{10,11... | collective-permute-start | bytes 786440 | tf_op jit(solution)/shard_map/ppermute | solution.py:64
  224.8 43.5 %collective-permute-start.13 = (bf16[4,1,3,64,1024]{4,3,2,0,1:T(8,128)(2,1)}, bf16[4,1,3,64,1024]{4,3,2,0,1:T(8,128)(2,1)}, u32[]{:S(2)}, u32[]{:S(2)}) collective-permute-start(bf16[4,1,3,64,1024]{4,3,2,0,1:T(8,128)(2,1)} %fusion.16), channel_id=1, source_target_pairs={{0,4},{2,6},{4,0},{6,2},{1,5},{3,7},{5,1},{7,3},{8,12},{10,14},{12... | collective-permute-start | bytes 4718600 | tf_op jit(solution)/shard_map/ppermute | solution.py:64
  239.0 14.8 %collective-permute-start.27 = (bf16[4,2,64,512]{3,2,1,0:T(8,128)(2,1)}, bf16[4,2,64,512]{3,2,1,0:T(8,128)(2,1)}, u32[]{:S(2)}, u32[]{:S(2)}) collective-permute-start(bf16[4,2,64,512]{3,2,1,0:T(8,128)(2,1)} %fusion.36), channel_id=1, source_target_pairs={{0,2},{2,0},{4,6},{6,4},{1,3},{3,1},{5,7},{7,5},{8,10},{10,8},{12,... | collective-permute-start | bytes 1572872 | tf_op jit(solution)/shard_map/ppermute | solution.py:64
  255.6 10.8 %collective-permute-start.28 = (bf16[4,1,64,512]{3,2,0,1:T(8,128)(2,1)S(1)}, bf16[4,1,64,512]{3,2,0,1:T(8,128)(2,1)S(1)}, u32[]{:S(2)}, u32[]{:S(2)}) collective-permute-start(bf16[4,1,64,512]{3,2,0,1:T(8,128)(2,1)S(1)} %fusion.55), channel_id=1, source_target_pairs={{0,4},{2,6},{4,0},{6,2},{1,5},{3,7},{5,1},{7,3},{8,12},{10,14},{12... | collective-permute-start | bytes 786440 | tf_op jit(solution)/shard_map/ppermute | solution.py:64
  281.1 54.2 %all-to-all-start.3 = ((bf16[4,3,64,1024]{3,2,1,0:T(8,128)(2,1)}), bf16[4,3,64,1024]{3,2,1,0:T(8,128)(2,1)}, u32[]{:S(2)}, u32[]{:S(2)}) async-start(bf16[4,3,64,1024]{3,2,1,0:T(8,128)(2,1)} %fusion.17), calls=%async_computation.3 | async-start | bytes 3145728 | tf_op jit(solution)/shard_map/all_to_all | solution.py:317
  296.3 9.3 %collective-permute-start.17 = (bf16[128,1024]{1,0:T(8,128)(2,1)S(1)}, bf16[128,1024]{1,0:T(8,128)(2,1)S(1)}, u32[]{:S(2)}, u32[]{:S(2)}) collective-permute-start(bf16[128,1024]{1,0:T(8,128)(2,1)S(1)} %get-tuple-element.99), channel_id=1, source_target_pairs={{0,1},{1,0},{2,3},{3,2},{4,5},{5,4},{6,7},{7,6},{8,9},{9,8},{10,11... | collective-permute-start | bytes 786440 | tf_op jit(solution)/shard_map/ppermute | solution.py:64
  298.4 11.2 %collective-permute-start.16 = (bf16[128,1024]{1,0:T(8,128)(2,1)S(1)}, bf16[128,1024]{1,0:T(8,128)(2,1)S(1)}, u32[]{:S(2)}, u32[]{:S(2)}) collective-permute-start(bf16[128,1024]{1,0:T(8,128)(2,1)S(1)} %reduce-precision_convert_fusion.1), channel_id=1, source_target_pairs={{0,1},{1,0},{2,3},{3,2},{4,5},{5,4},{6,7},{7,6},{8,9},{9,8},{10,11... | collective-permute-start | bytes 786440 | tf_op jit(solution)/shard_map/ppermute | solution.py:64
  308.3 12.2 %collective-permute-start.23 = (bf16[4,2,64,1024]{3,2,1,0:T(8,128)(2,1)S(1)}, bf16[4,2,64,1024]{3,2,1,0:T(8,128)(2,1)S(1)}, u32[]{:S(2)}, u32[]{:S(2)}) collective-permute-start(bf16[4,2,64,1024]{3,2,1,0:T(8,128)(2,1)S(1)} %fusion.21), channel_id=1, source_target_pairs={{0,2},{2,0},{4,6},{6,4},{1,3},{3,1},{5,7},{7,5},{8,10},{10,8},{12,... | collective-permute-start | bytes 3145736 | tf_op jit(solution)/shard_map/ppermute | solution.py:64
  321.4 12.0 %collective-permute-start.24 = (bf16[4,1,64,1024]{3,2,0,1:T(8,128)(2,1)S(1)}, bf16[4,1,64,1024]{3,2,0,1:T(8,128)(2,1)S(1)}, u32[]{:S(2)}, u32[]{:S(2)}) collective-permute-start(bf16[4,1,64,1024]{3,2,0,1:T(8,128)(2,1)S(1)} %fusion.35), channel_id=1, source_target_pairs={{0,4},{2,6},{4,0},{6,2},{1,5},{3,7},{5,1},{7,3},{8,12},{10,14},{12... | collective-permute-start | bytes 1572872 | tf_op jit(solution)/shard_map/ppermute | solution.py:64
  341.1 7.6 %collective-permute-start.26 = (bf16[1,64,1024]{2,1,0:T(8,128)(2,1)S(1)}, bf16[1,64,1024]{2,1,0:T(8,128)(2,1)S(1)}, u32[]{:S(2)}, u32[]{:S(2)}) collective-permute-start(bf16[1,64,1024]{2,1,0:T(8,128)(2,1)S(1)} %fusion.63), channel_id=1, source_target_pairs={{0,16},{8,24},{16,0},{24,8},{1,17},{9,25},{17,1},{25,9},{2,18},{10... | collective-permute-start | bytes 393224 | tf_op jit(solution)/shard_map/ppermute | solution.py:64
  (74 other events, 480.2 us)
Sparse Core Ops, SparseCore 0:
  136.3 28.3 all-gather.1

commit v4 on v3

--- a/solution.py
+++ b/solution.py
@@ -188,26 +188,26 @@
     full = packed_all[None]
     for bit in reversed(bits[1:]):
         full = ordered_step(full, "context", bit)
-    full, owner, early = tie(full, owner, early)
     full = ordered_step(full, "context", 1)
     full = jnp.swapaxes(full, 0, 1).reshape(model_width, packed.shape[1])
     qkv_full = full[:, :qkv_cols]
     output_full = full[:, qkv_cols : qkv_cols + q_cols]
     gain_rows = full[:, qkv_cols + q_cols :].astype(f32).T
     gain_attn, gain_ffn = gain_rows[0], gain_rows[1]
+
+    context_index = lax.axis_index("context")
+    positions = context_index * length + jnp.arange(length, dtype=jnp.int32)
+    cosine_table, rotary_sine_values = rope_tables(positions, HEAD_DIM)
+    scale_one = inverse_rms(tokens)
+    normed_one = (tokens * scale_one * gain_attn).astype(b16)
+    qkv_lin = jnp.dot(normed_one, qkv_full, preferred_element_type=f32)
+    qkv_lin, owner, early = tie(qkv_lin, owner, early)
     early_all = early[None]
     for bit in reversed(axis_bits("shard")):
         early_all = ordered_step(early_all, "shard", bit)
     expert_blocks = owner[None]
     for bit in reversed(bits[1:]):
         expert_blocks = ordered_step(expert_blocks, "context", bit)
-
-    context_index = lax.axis_index("context")
-    positions = context_index * length + jnp.arange(length, dtype=jnp.int32)
-    cosine_table, rotary_sine_values = rope_tables(positions, HEAD_DIM)
-    scale_one = inverse_rms(tokens)
-    normed_one = (tokens * scale_one * gain_attn).astype(b16)
-    qkv_lin = jnp.dot(normed_one, qkv_full, preferred_element_type=f32)
     turned = apply_rotary(
         qkv_lin[:, : q_cols + kv_cols].reshape(length, heads + kv_heads, HEAD_DIM),
         cosine_table,

time: 362 us -> 389 us (1.075)
  waiting for transfers between devices: 142 us -> 156 us
  local copies, waits for them, and re-layouts: 55.4 us -> 63.5 us
    all_to_all x1, waiting for transfers between devices: 15.7 us -> 30.3 us  [body(): lax.all_to_all(stacked_weights, 'shard', split_axis=0, concat_axis=0, til...]
    another operation x3, local copies, waits for them, and re-layouts: 0.6 us -> 5.3 us  [body(): stacked_weights = jnp.stack([gate_weight, up_weight, down_weight], axis=0)]
    unnamed x133 -> x129, local copies, waits for them, and re-layouts: 12.2 us -> 12.8 us
  transfers between devices with their start and end apart: 36 -> 36, of which waited for: 23 -> 23; matrix products, arithmetic and copies ran while one was open for 32% -> 30% of each run, Pallas kernels for 0% -> 0%
where the time goes in v4:
time: 389 us; the launch traced here: 383 us
  waiting for transfers between devices  156 us (40%)
  local copies, waits for them, and re-layouts  63.5 us (16%)
  other arithmetic  55.4 us (14%)
  starting transfers between devices  55.4 us (14%)
  matrix products  37 us (10%)
  between operations  15.6 us (4%)
    ppermute x31, waiting for transfers between devices, exchange(): return lax.ppermute(array, axis, [(i, i ^ bit) for i in range(size)])  96.3 us
    ppermute x31, starting transfers between devices, exchange(): return lax.ppermute(array, axis, [(i, i ^ bit) for i in range(size)])  34.8 us
    all_to_all x1, waiting for transfers between devices, body(): lax.all_to_all(stacked_weights, 'shard', split_axis=0, concat_axis=0, til...  30.3 us
    all_to_all x1, waiting for transfers between devices, body(): lax.all_to_all(normed_two_terms.reshape(shard_count, length, model_width)...  16.8 us
    all_gather x1, waiting for transfers between devices, body(): x_all = lax.all_gather(normed_two, 'shard', axis=0, tiled=True)  12.8 us
    unnamed x129, local copies, waits for them, and re-layouts  12.8 us
    another operation x12, other arithmetic, ordered_step(): return jnp.stack([low, high], axis=1).reshape((-1,) + blocks.shape[1:])  9.99 us
    dot_general x5, matrix products, contract_cols(): lax.dot_general(left, right, (((1,), (1,)), ((), ())), preferred_element_...  9.88 us
  transfers between devices with their start and end apart: 36, of which 23 were waited for; matrix products, arithmetic and copies ran while one was open for 30% of the time, Pallas kernels for 0%

profile of v4, /device:TPU:0, one launch (start us, length us, event | category | flops | bytes accessed | tf_op | source)
XLA Modules:
  0.0 383.1 jit_solution(17598353002626192589)
XLA Ops:
  11.2 4.1 %collective-permute-start = (bf16[1,64,1664]{2,1,0:T(8,128)(2,1)S(1)}, bf16[1,64,1664]{2,1,0:T(8,128)(2,1)S(1)}, u32[]{:S(2)}, u32[]{:S(2)}) collective-permute-start(bf16[1,64,1664]{2,1,0:T(8,128)(2,1)S(1)} %bitcast.544), channel_id=1, source_target_pairs={{0,16},{8,24},{16,0},{24,8},{1,17},{9,25},{17,1},{25,9},{2,18},{10... | collective-permute-start | bytes 638984 | tf_op jit(solution)/shard_map/ppermute | solution.py:64
  15.3 9.8 %collective-permute-done = bf16[1,64,1664]{2,1,0:T(8,128)(2,1)S(1)} collective-permute-done((bf16[1,64,1664]{2,1,0:T(8,128)(2,1)S(1)}, bf16[1,64,1664]{2,1,0:T(8,128)(2,1)S(1)}, u32[]{:S(2)}, u32[]{:S(2)}) %collective-permute-start) | collective-permute-done | bytes 213024 | tf_op jit(solution)/shard_map/ppermute | solution.py:64
  26.0 10.3 %collective-permute-done.1 = bf16[2,64,1664]{2,1,0:T(8,128)(2,1)S(1)} collective-permute-done((bf16[2,64,1664]{2,1,0:T(8,128)(2,1)S(1)}, bf16[2,64,1664]{2,1,0:T(8,128)(2,1)S(1)}, u32[]{:S(2)}, u32[]{:S(2)}) %collective-permute-start.1) | collective-permute-done | bytes 426016 | tf_op jit(solution)/shard_map/ppermute | solution.py:64
  43.1 12.7 %collective-permute-done.2 = bf16[1,4,64,1664]{3,2,1,0:T(8,128)(2,1)S(1)} collective-permute-done((bf16[1,4,64,1664]{3,2,1,0:T(8,128)(2,1)S(1)}, bf16[1,4,64,1664]{3,2,1,0:T(8,128)(2,1)S(1)}, u32[]{:S(2)}, u32[]{:S(2)}) %collective-permute-start.2) | collective-permute-done | bytes 852000 | tf_op jit(solution)/shard_map/ppermute | solution.py:64
  62.4 6.5 %all-to-all-start = ((bf16[4,3,64,1024]{3,2,1,0:T(8,128)(2,1)}), bf16[4,3,64,1024]{3,2,1,0:T(8,128)(2,1)}, u32[]{:S(2)}, u32[]{:S(2)}) async-start(bf16[4,3,64,1024]{3,2,1,0:T(8,128)(2,1)} %copy.349), calls=%async_computation | async-start | bytes 3145728 | tf_op jit(solution)/shard_map/all_to_all | solution.py:186
  76.3 30.3 %all-to-all-done = bf16[4,3,64,1024]{3,2,1,0:T(8,128)(2,1)} async-done(((bf16[4,3,64,1024]{3,2,1,0:T(8,128)(2,1)}), bf16[4,3,64,1024]{3,2,1,0:T(8,128)(2,1)}, u32[]{:S(2)}, u32[]{:S(2)}) %all-to-all-start) | async-done | bytes 1572896 | tf_op jit(solution)/shard_map/all_to_all | solution.py:186
  117.2 3.5 collective-permute-done.4
  139.5 3.6 collective-permute-done.6
  144.9 9.9 %collective-permute-done.9 = bf16[2,128,1152]{2,1,0:T(8,128)(2,1)S(1)} collective-permute-done((bf16[2,128,1152]{2,1,0:T(8,128)(2,1)S(1)}, bf16[2,128,1152]{2,1,0:T(8,128)(2,1)S(1)}, u32[]{:S(2)}, u32[]{:S(2)}) %collective-permute-start.9) | collective-permute-done | bytes 589856 | tf_op jit(solution)/shard_map/ppermute | solution.py:64
  156.2 3.6 collective-permute-done.7
  164.6 3.4 collective-permute-done.10
  177.9 12.8 %all-gather.2.cloned.1.call-done = bf16[512,1024]{1,0:T(8,128)(2,1)} async-done(((bf16[128,1024]{1,0:T(8,128)(2,1)}), bf16[512,1024]{1,0:T(8,128)(2,1)}) %all-gather.2.cloned.1.call-update) | async-done | bytes 1048592 | tf_op jit(solution)/shard_map/all_gather | solution.py:249
  190.7 3.5 fusion.97
  208.8 4.7 %all-to-all-start.1 = ((bf16[4,128,1024]{2,1,0:T(8,128)(2,1)}), bf16[4,128,1024]{2,1,0:T(8,128)(2,1)}, u32[]{:S(2)}, u32[]{:S(2)}) async-start(bf16[4,128,1024]{2,1,0:T(8,128)(2,1)} %bitcast.62), calls=%async_computation.1 | async-start | bytes 2097152 | tf_op jit(solution)/shard_map/all_to_all | solution.py:269
  213.6 4.0 %convolution_convert_fusion.2 = bf16[512,1024]{1,0:T(8,128)(2,1)} fusion(bf16[512,1024]{1,0:T(8,128)(2,1)S(1)} %copy-done.57, bf16[1024,1024]{1,0:T(8,128)(2,1)} %bitcast.513), kind=kOutput, calls=%fused_computation.54 | convolution fusion | flops 1074266112 | bytes 4194304 | tf_op jit(solution)/shard_map/dot_general | solution.py:57
  217.6 5.8 %fusion.1 = bf16[4,2,3,64,1024]{4,3,2,1,0:T(8,128)(2,1)} fusion(bf16[4,2,3,64,1024]{4,3,2,1,0:T(8,128)(2,1)} %collective-permute-done.11, pred[]{:T(512)S(6)} %eq.39, bf16[4,2,2,3,64,1024]{5,4,3,2,1,0:T(8,128)(2,1)S(1)} %bitcast.491), kind=kLoop, calls=%fused_computation.4 | loop fusion | flops 7864320 | bytes 12582913 | tf_op jit(solution)/shard_map/convert_element_type | solution.py:285
  223.4 16.8 %all-to-all-done.1 = bf16[4,128,1024]{2,1,0:T(8,128)(2,1)} async-done(((bf16[4,128,1024]{2,1,0:T(8,128)(2,1)}), bf16[4,128,1024]{2,1,0:T(8,128)(2,1)}, u32[]{:S(2)}, u32[]{:S(2)}) %all-to-all-start.1) | async-done | bytes 1048608 | tf_op jit(solution)/shard_map/all_to_all | solution.py:269
  242.5 4.3 %all-to-all-start.2 = ((bf16[4,128,1024]{2,1,0:T(8,128)(2,1)}), bf16[4,128,1024]{2,1,0:T(8,128)(2,1)}, u32[]{:S(2)}, u32[]{:S(2)}) async-start(bf16[4,128,1024]{2,1,0:T(8,128)(2,1)} %bitcast.536), calls=%async_computation.2 | async-start | bytes 2097152 | tf_op jit(solution)/shard_map/all_to_all | solution.py:287
  252.3 3.6 collective-permute-done.12
  284.1 8.2 %collective-permute-done.28 = bf16[4,1,64,512]{3,2,0,1:T(8,128)(2,1)S(1)} collective-permute-done((bf16[4,1,64,512]{3,2,0,1:T(8,128)(2,1)S(1)}, bf16[4,1,64,512]{3,2,0,1:T(8,128)(2,1)S(1)}, u32[]{:S(2)}, u32[]{:S(2)}) %collective-permute-start.28) | collective-permute-done | bytes 262176 | tf_op jit(solution)/shard_map/ppermute | solution.py:64
  294.3 3.6 fusion.17
  307.1 4.6 %all-to-all-start.3 = ((bf16[4,3,64,1024]{3,2,1,0:T(8,128)(2,1)}), bf16[4,3,64,1024]{3,2,1,0:T(8,128)(2,1)}, u32[]{:S(2)}, u32[]{:S(2)}) async-start(bf16[4,3,64,1024]{3,2,1,0:T(8,128)(2,1)} %fusion.17), calls=%async_computation.3 | async-start | bytes 3145728 | tf_op jit(solution)/shard_map/all_to_all | solution.py:317
  325.9 5.7 %collective-permute-done.17 = bf16[128,1024]{1,0:T(8,128)(2,1)S(1)} collective-permute-done((bf16[128,1024]{1,0:T(8,128)(2,1)S(1)}, bf16[128,1024]{1,0:T(8,128)(2,1)S(1)}, u32[]{:S(2)}, u32[]{:S(2)}) %collective-permute-start.17) | collective-permute-done | bytes 262176 | tf_op jit(solution)/shard_map/ppermute | solution.py:64
  353.0 6.4 %collective-permute-done.24 = bf16[4,1,64,1024]{3,2,0,1:T(8,128)(2,1)S(1)} collective-permute-done((bf16[4,1,64,1024]{3,2,0,1:T(8,128)(2,1)S(1)}, bf16[4,1,64,1024]{3,2,0,1:T(8,128)(2,1)S(1)}, u32[]{:S(2)}, u32[]{:S(2)}) %collective-permute-start.24) | collective-permute-done | bytes 524320 | tf_op jit(solution)/shard_map/ppermute | solution.py:64
  (347 shorter events, 185.9 us)
Async XLA Ops:
  11.2 13.9 %collective-permute-start = (bf16[1,64,1664]{2,1,0:T(8,128)(2,1)S(1)}, bf16[1,64,1664]{2,1,0:T(8,128)(2,1)S(1)}, u32[]{:S(2)}, u32[]{:S(2)}) collective-permute-start(bf16[1,64,1664]{2,1,0:T(8,128)(2,1)S(1)} %bitcast.544), channel_id=1, source_target_pairs={{0,16},{8,24},{16,0},{24,8},{1,17},{9,25},{17,1},{25,9},{2,18},{10... | collective-permute-start | bytes 638984 | tf_op jit(solution)/shard_map/ppermute | solution.py:64
  25.2 11.1 %collective-permute-start.1 = (bf16[2,64,1664]{2,1,0:T(8,128)(2,1)S(1)}, bf16[2,64,1664]{2,1,0:T(8,128)(2,1)S(1)}, u32[]{:S(2)}, u32[]{:S(2)}) collective-permute-start(bf16[2,64,1664]{2,1,0:T(8,128)(2,1)S(1)} %maximum_bitcast_fusion.4), channel_id=1, source_target_pairs={{0,8},{8,0},{16,24},{24,16},{1,9},{9,1},{17,25},{25,17},{2,10},{10... | collective-permute-start | bytes 1277960 | tf_op jit(solution)/shard_map/ppermute | solution.py:64
  36.5 19.3 %collective-permute-start.2 = (bf16[1,4,64,1664]{3,2,1,0:T(8,128)(2,1)S(1)}, bf16[1,4,64,1664]{3,2,1,0:T(8,128)(2,1)S(1)}, u32[]{:S(2)}, u32[]{:S(2)}) collective-permute-start(bf16[1,4,64,1664]{3,2,1,0:T(8,128)(2,1)S(1)} %bitcast.506), channel_id=1, source_target_pairs={{0,4},{2,6},{4,0},{6,2},{1,5},{3,7},{5,1},{7,3},{8,12},{10,14},{12... | collective-permute-start | bytes 2555912 | tf_op jit(solution)/shard_map/ppermute | solution.py:64
  59.4 12.1 %collective-permute-start.3 = (bf16[2,4,64,1664]{3,2,1,0:T(8,128)(2,1)}, bf16[2,4,64,1664]{3,2,1,0:T(8,128)(2,1)}, u32[]{:S(2)}, u32[]{:S(2)}) collective-permute-start(bf16[2,4,64,1664]{3,2,1,0:T(8,128)(2,1)} %maximum_bitcast_fusion.1), channel_id=1, source_target_pairs={{0,2},{2,0},{4,6},{6,4},{1,3},{3,1},{5,7},{7,5},{8,10},{10,8},{12,... | collective-permute-start | bytes 5111816 | tf_op jit(solution)/shard_map/ppermute | solution.py:64
  62.4 44.2 %all-to-all-start = ((bf16[4,3,64,1024]{3,2,1,0:T(8,128)(2,1)}), bf16[4,3,64,1024]{3,2,1,0:T(8,128)(2,1)}, u32[]{:S(2)}, u32[]{:S(2)}) async-start(bf16[4,3,64,1024]{3,2,1,0:T(8,128)(2,1)} %copy.349), calls=%async_computation | async-start | bytes 3145728 | tf_op jit(solution)/shard_map/all_to_all | solution.py:186
  68.9 121.8 %all-gather.2.cloned.1.call-start = ((), (), s32[]{:S(2)}) async-start(), calls=%async_computation.4 | async-start | bytes 1310720 | tf_op jit(solution)/shard_map/all_gather | solution.py:249
  122.5 15.8 %collective-permute-start.8 = (bf16[1,128,1152]{2,1,0:T(8,128)(2,1)}, bf16[1,128,1152]{2,1,0:T(8,128)(2,1)}, u32[]{:S(2)}, u32[]{:S(2)}) collective-permute-start(bf16[1,128,1152]{2,1,0:T(8,128)(2,1)} %bitcast.529), channel_id=1, source_target_pairs={{0,16},{8,24},{16,0},{24,8},{1,17},{9,25},{17,1},{25,9},{2,18},{10... | collective-permute-start | bytes 884744 | tf_op jit(solution)/shard_map/ppermute | solution.py:64
  122.6 37.2 %collective-permute-start.7 = (bf16[1,4,3,64,1024]{4,3,2,1,0:T(8,128)(2,1)}, bf16[1,4,3,64,1024]{4,3,2,1,0:T(8,128)(2,1)}, u32[]{:S(2)}, u32[]{:S(2)}) collective-permute-start(bf16[1,4,3,64,1024]{4,3,2,1,0:T(8,128)(2,1)} %bitcast.41), channel_id=1, source_target_pairs={{0,4},{2,6},{4,0},{6,2},{1,5},{3,7},{5,1},{7,3},{8,12},{10,14},{12... | collective-permute-start | bytes 4718600 | tf_op jit(solution)/shard_map/ppermute | solution.py:64
  134.6 8.5 %collective-permute-start.6 = (bf16[128,1024]{1,0:T(8,128)(2,1)S(1)}, bf16[128,1024]{1,0:T(8,128)(2,1)S(1)}, u32[]{:S(2)}, u32[]{:S(2)}) collective-permute-start(bf16[128,1024]{1,0:T(8,128)(2,1)S(1)} %get-tuple-element.97), channel_id=1, source_target_pairs={{0,1},{1,0},{2,3},{3,2},{4,5},{5,4},{6,7},{7,6},{8,9},{9,8},{10,11... | collective-permute-start | bytes 786440 | tf_op jit(solution)/shard_map/ppermute | solution.py:64
  139.4 15.4 %collective-permute-start.9 = (bf16[2,128,1152]{2,1,0:T(8,128)(2,1)S(1)}, bf16[2,128,1152]{2,1,0:T(8,128)(2,1)S(1)}, u32[]{:S(2)}, u32[]{:S(2)}) collective-permute-start(bf16[2,128,1152]{2,1,0:T(8,128)(2,1)S(1)} %maximum_bitcast_fusion.3), channel_id=1, source_target_pairs={{0,8},{8,0},{16,24},{24,16},{1,9},{9,1},{17,25},{25,17},{2,10},{10... | collective-permute-start | bytes 1769480 | tf_op jit(solution)/shard_map/ppermute | solution.py:64
  205.2 12.4 %collective-permute-start.11 = (bf16[4,2,3,64,1024]{4,3,2,1,0:T(8,128)(2,1)}, bf16[4,2,3,64,1024]{4,3,2,1,0:T(8,128)(2,1)}, u32[]{:S(2)}, u32[]{:S(2)}) collective-permute-start(bf16[4,2,3,64,1024]{4,3,2,1,0:T(8,128)(2,1)} %fusion.2), channel_id=1, source_target_pairs={{0,2},{2,0},{4,6},{6,4},{1,3},{3,1},{5,7},{7,5},{8,10},{10,8},{12,... | collective-permute-start | bytes 9437192 | tf_op jit(solution)/shard_map/ppermute | solution.py:64
  208.8 31.5 %all-to-all-start.1 = ((bf16[4,128,1024]{2,1,0:T(8,128)(2,1)}), bf16[4,128,1024]{2,1,0:T(8,128)(2,1)}, u32[]{:S(2)}, u32[]{:S(2)}) async-start(bf16[4,128,1024]{2,1,0:T(8,128)(2,1)} %bitcast.62), calls=%async_computation.1 | async-start | bytes 2097152 | tf_op jit(solution)/shard_map/all_to_all | solution.py:269
  242.5 64.6 %all-to-all-start.2 = ((bf16[4,128,1024]{2,1,0:T(8,128)(2,1)}), bf16[4,128,1024]{2,1,0:T(8,128)(2,1)}, u32[]{:S(2)}, u32[]{:S(2)}) async-start(bf16[4,128,1024]{2,1,0:T(8,128)(2,1)} %bitcast.536), calls=%async_computation.2 | async-start | bytes 2097152 | tf_op jit(solution)/shard_map/all_to_all | solution.py:287
  247.9 8.0 %collective-permute-start.12 = (bf16[128,1024]{1,0:T(8,128)(2,1)S(1)}, bf16[128,1024]{1,0:T(8,128)(2,1)S(1)}, u32[]{:S(2)}, u32[]{:S(2)}) collective-permute-start(bf16[128,1024]{1,0:T(8,128)(2,1)S(1)} %reduce-precision_convert_fusion.2), channel_id=1, source_target_pairs={{0,1},{1,0},{2,3},{3,2},{4,5},{5,4},{6,7},{7,6},{8,9},{9,8},{10,11... | collective-permute-start | bytes 786440 | tf_op jit(solution)/shard_map/ppermute | solution.py:64
  250.8 43.5 %collective-permute-start.13 = (bf16[4,1,3,64,1024]{4,3,2,0,1:T(8,128)(2,1)}, bf16[4,1,3,64,1024]{4,3,2,0,1:T(8,128)(2,1)}, u32[]{:S(2)}, u32[]{:S(2)}) collective-permute-start(bf16[4,1,3,64,1024]{4,3,2,0,1:T(8,128)(2,1)} %fusion.16), channel_id=1, source_target_pairs={{0,4},{2,6},{4,0},{6,2},{1,5},{3,7},{5,1},{7,3},{8,12},{10,14},{12... | collective-permute-start | bytes 4718600 | tf_op jit(solution)/shard_map/ppermute | solution.py:64
  264.9 14.8 %collective-permute-start.27 = (bf16[4,2,64,512]{3,2,1,0:T(8,128)(2,1)}, bf16[4,2,64,512]{3,2,1,0:T(8,128)(2,1)}, u32[]{:S(2)}, u32[]{:S(2)}) collective-permute-start(bf16[4,2,64,512]{3,2,1,0:T(8,128)(2,1)} %fusion.36), channel_id=1, source_target_pairs={{0,2},{2,0},{4,6},{6,4},{1,3},{3,1},{5,7},{7,5},{8,10},{10,8},{12,... | collective-permute-start | bytes 1572872 | tf_op jit(solution)/shard_map/ppermute | solution.py:64
  281.6 10.8 %collective-permute-start.28 = (bf16[4,1,64,512]{3,2,0,1:T(8,128)(2,1)S(1)}, bf16[4,1,64,512]{3,2,0,1:T(8,128)(2,1)S(1)}, u32[]{:S(2)}, u32[]{:S(2)}) collective-permute-start(bf16[4,1,64,512]{3,2,0,1:T(8,128)(2,1)S(1)} %fusion.55), channel_id=1, source_target_pairs={{0,4},{2,6},{4,0},{6,2},{1,5},{3,7},{5,1},{7,3},{8,12},{10,14},{12... | collective-permute-start | bytes 786440 | tf_op jit(solution)/shard_map/ppermute | solution.py:64
  298.1 6.6 %collective-permute-start.30 = (bf16[1,64,512]{2,1,0:T(8,128)(2,1)S(1)}, bf16[1,64,512]{2,1,0:T(8,128)(2,1)S(1)}, u32[]{:S(2)}, u32[]{:S(2)}) collective-permute-start(bf16[1,64,512]{2,1,0:T(8,128)(2,1)S(1)} %fusion.67), channel_id=1, source_target_pairs={{0,16},{8,24},{16,0},{24,8},{1,17},{9,25},{17,1},{25,9},{2,18},{10... | collective-permute-start | bytes 196616 | tf_op jit(solution)/shard_map/ppermute | solution.py:64
  307.1 54.2 %all-to-all-start.3 = ((bf16[4,3,64,1024]{3,2,1,0:T(8,128)(2,1)}), bf16[4,3,64,1024]{3,2,1,0:T(8,128)(2,1)}, u32[]{:S(2)}, u32[]{:S(2)}) async-start(bf16[4,3,64,1024]{3,2,1,0:T(8,128)(2,1)} %fusion.17), calls=%async_computation.3 | async-start | bytes 3145728 | tf_op jit(solution)/shard_map/all_to_all | solution.py:317
  322.3 9.3 %collective-permute-start.17 = (bf16[128,1024]{1,0:T(8,128)(2,1)S(1)}, bf16[128,1024]{1,0:T(8,128)(2,1)S(1)}, u32[]{:S(2)}, u32[]{:S(2)}) collective-permute-start(bf16[128,1024]{1,0:T(8,128)(2,1)S(1)} %get-tuple-element.99), channel_id=1, source_target_pairs={{0,1},{1,0},{2,3},{3,2},{4,5},{5,4},{6,7},{7,6},{8,9},{9,8},{10,11... | collective-permute-start | bytes 786440 | tf_op jit(solution)/shard_map/ppermute | solution.py:64
  324.4 11.2 %collective-permute-start.16 = (bf16[128,1024]{1,0:T(8,128)(2,1)S(1)}, bf16[128,1024]{1,0:T(8,128)(2,1)S(1)}, u32[]{:S(2)}, u32[]{:S(2)}) collective-permute-start(bf16[128,1024]{1,0:T(8,128)(2,1)S(1)} %reduce-precision_convert_fusion.1), channel_id=1, source_target_pairs={{0,1},{1,0},{2,3},{3,2},{4,5},{5,4},{6,7},{7,6},{8,9},{9,8},{10,11... | collective-permute-start | bytes 786440 | tf_op jit(solution)/shard_map/ppermute | solution.py:64
  334.3 12.2 %collective-permute-start.23 = (bf16[4,2,64,1024]{3,2,1,0:T(8,128)(2,1)S(1)}, bf16[4,2,64,1024]{3,2,1,0:T(8,128)(2,1)S(1)}, u32[]{:S(2)}, u32[]{:S(2)}) collective-permute-start(bf16[4,2,64,1024]{3,2,1,0:T(8,128)(2,1)S(1)} %fusion.21), channel_id=1, source_target_pairs={{0,2},{2,0},{4,6},{6,4},{1,3},{3,1},{5,7},{7,5},{8,10},{10,8},{12,... | collective-permute-start | bytes 3145736 | tf_op jit(solution)/shard_map/ppermute | solution.py:64
  347.3 12.0 %collective-permute-start.24 = (bf16[4,1,64,1024]{3,2,0,1:T(8,128)(2,1)S(1)}, bf16[4,1,64,1024]{3,2,0,1:T(8,128)(2,1)S(1)}, u32[]{:S(2)}, u32[]{:S(2)}) collective-permute-start(bf16[4,1,64,1024]{3,2,0,1:T(8,128)(2,1)S(1)} %fusion.35), channel_id=1, source_target_pairs={{0,4},{2,6},{4,0},{6,2},{1,5},{3,7},{5,1},{7,3},{8,12},{10,14},{12... | collective-permute-start | bytes 1572872 | tf_op jit(solution)/shard_map/ppermute | solution.py:64
  367.0 7.6 %collective-permute-start.26 = (bf16[1,64,1024]{2,1,0:T(8,128)(2,1)S(1)}, bf16[1,64,1024]{2,1,0:T(8,128)(2,1)S(1)}, u32[]{:S(2)}, u32[]{:S(2)}) collective-permute-start(bf16[1,64,1024]{2,1,0:T(8,128)(2,1)S(1)} %fusion.63), channel_id=1, source_target_pairs={{0,16},{8,24},{16,0},{24,8},{1,17},{9,25},{17,1},{25,9},{2,18},{10... | collective-permute-start | bytes 393224 | tf_op jit(solution)/shard_map/ppermute | solution.py:64
  (72 other events, 501.0 us)
Sparse Core Ops, SparseCore 0:
  162.4 28.2 all-gather.1
